TPU v7x, 32 devices: a whole 2x2x4 slice. The times are simulated.
32 devices in a mesh: dp: 8 (over z, y), tensor: 4 (over x, core).
Axes of the slice: x: 2, y: 2, z: 4, core: 2. Of those that a mesh axis runs over, the one named last changes fastest.
Arguments:
- hidden_in: bfloat16 [256, 8192], P('dp'), may hold values from -40 to 40
- norm_gain: bfloat16 [8192], P('dp'), may hold values from 0.25 to 2.5
- query_weight: bfloat16 [8192, 8192], P('dp', 'tensor'), may hold values from -0.0625 to 0.0625
- key_weight: bfloat16 [8192, 1024], P('dp', 'tensor'), may hold values from -0.0625 to 0.0625
- value_weight: bfloat16 [8192, 1024], P('dp', 'tensor'), may hold values from -0.0625 to 0.0625
- output_weight: bfloat16 [8192, 8192], P('tensor', 'dp'), may hold values from -0.25 to 0.25
- key_value_cache: bfloat16 [256, 256, 2, 8, 128], P('dp', None, None, 'tensor'), may hold values from -150 to 150, as said below
- cache_lengths: int32 [256], replicated, may hold values from 2 to 256, as said below
- parent_beam: int32 [256], replicated, may hold values from 0 to 255, as said below
- beam_alive: int32 [256], replicated, may hold values 0 or 1
Outputs:
- attention_out: bfloat16 [256, 8192], P(None, 'dp')
Inputs may be any that keep to these rules, and one draw needn't show every extreme that they name: `parent_beam`: among the beams of one device, at most 8 have parents that lie on any one device (beam i lies on device i // 32); on every device some device holds exactly 8 of their parents. `cache_lengths`: some beam holds exactly 256 tokens. `key_value_cache`: slots at or past a beam's length hold arbitrary values.
All inputs are finite; a program needn't handle non-finite values.
Results may differ from a plain program's by a relative error of at most 0.012.
Values may be sent and summed in bfloat16 or wider, within the bound.
A program may use at most 128 MiB of HBM per device.

v0:
```python
import math

import jax
import jax.numpy as jnp
from jax import lax
from jax.sharding import PartitionSpec as P

HEAD_DIM = 128


def rotate(vectors, position):
    half_width = vectors.shape[-1] // 2
    pair_index = jnp.arange(half_width).astype(jnp.float32)
    frequency = jnp.exp(pair_index * (-2.0 * math.log(1000000.0) / vectors.shape[-1]))
    angles = position.astype(jnp.float32)[:, None] * frequency[None, :]
    cosine = jnp.cos(angles)[:, None, :]
    sine_part = jnp.sin(angles)[:, None, :]
    first_half = vectors[..., :half_width]
    second = vectors[..., half_width:]
    return jnp.concatenate(
        [first_half * cosine - second * sine_part, second * cosine + first_half * sine_part],
        axis=-1,
    )


def attend(queries, key_rows, value_rows, key_new, value_new, length_row):
    row_count, head_total, head_width = queries.shape
    groups = key_rows.shape[2]
    length = key_rows.shape[1]
    grouped = queries.reshape(row_count, groups, head_total // groups, head_width)
    score_scale = 1.0 / math.sqrt(head_width)
    cached = (
        jnp.einsum("rkgd,rlkd->rkgl", grouped, key_rows, preferred_element_type=jnp.float32)
        * score_scale
    )
    latest = (
        jnp.einsum("rkgd,rkd->rkg", grouped, key_new, preferred_element_type=jnp.float32)
        * score_scale
    )
    is_valid = (jnp.arange(length, dtype=jnp.int32)[None, :] < length_row[:, None])[
        :, None, None, :
    ]
    cached = jnp.where(is_valid, cached, -jnp.inf)
    highest = jnp.maximum(jnp.max(cached, axis=-1), latest)
    cached_exp = jnp.exp(cached - highest[..., None])
    latest_exp = jnp.exp(latest - highest)
    denominator = jnp.sum(cached_exp, axis=-1) + latest_exp
    cached_weight = (cached_exp / denominator[..., None]).astype(jnp.bfloat16)
    latest_weight = (latest_exp / denominator).astype(jnp.bfloat16)
    mixture = jnp.einsum(
        "rkgl,rlkd->rkgd", cached_weight, value_rows, preferred_element_type=jnp.float32
    )
    mixture = (
        mixture
        + latest_weight.astype(jnp.float32)[..., None]
        * value_new.astype(jnp.float32)[:, :, None, :]
    )
    return mixture.reshape(row_count, head_total * head_width).astype(jnp.bfloat16)


def arrival_ranks(sources):
    ordinal = jnp.arange(sources.shape[-1], dtype=jnp.int32)
    earlier = (sources[..., None, :] == sources[..., :, None]) & (
        ordinal[None, :] < ordinal[:, None]
    )
    return jnp.sum(earlier.astype(jnp.int32), axis=-1)


def body(
    hidden_in,
    norm_gain,
    query_weight,
    key_weight,
    value_weight,
    output_weight,
    key_value_cache,
    cache_lengths,
    parent_beam,
    beam_alive,
):
    device_count = lax.axis_size("dp")
    device_rank = lax.axis_index("dp")
    local_beams = hidden_in.shape[0]
    capacity = max(2, (2 * local_beams + device_count - 1) // device_count)
    hidden_float = hidden_in.astype(jnp.float32)
    inverse = lax.rsqrt(jnp.mean(hidden_float * hidden_float, axis=1) + 1e-06)
    blocked = lax.all_to_all(hidden_in, "dp", split_axis=1, concat_axis=0, tiled=True)
    scaled = (blocked.astype(jnp.float32) * norm_gain.astype(jnp.float32)[None, :]).astype(
        jnp.bfloat16
    )
    query_width = query_weight.shape[1]
    key_width = key_weight.shape[1]
    summed = (
        lax.psum_scatter(
            jnp.concatenate(
                [
                    jnp.dot(scaled, query_weight, preferred_element_type=jnp.float32),
                    jnp.dot(scaled, key_weight, preferred_element_type=jnp.float32),
                    jnp.dot(scaled, value_weight, preferred_element_type=jnp.float32),
                ],
                axis=1,
            ),
            "dp",
            scatter_dimension=0,
            tiled=True,
        )
        * inverse[:, None]
    )
    first_beam = device_rank * local_beams
    my_parent = lax.dynamic_slice_in_dim(parent_beam, first_beam, local_beams)
    my_alive = lax.dynamic_slice_in_dim(beam_alive, first_beam, local_beams)
    position = jnp.take(cache_lengths, my_parent)
    head_count = query_width // HEAD_DIM
    group_count = key_width // HEAD_DIM
    queries = rotate(
        summed[:, :query_width].reshape(local_beams, head_count, HEAD_DIM), position
    ).astype(jnp.bfloat16)
    key_new = rotate(
        summed[:, query_width : query_width + key_width].reshape(
            local_beams, group_count, HEAD_DIM
        ),
        position,
    ).astype(jnp.bfloat16)
    value_new = (
        summed[:, query_width + key_width :]
        .reshape(local_beams, group_count, HEAD_DIM)
        .astype(jnp.bfloat16)
    )
    source = my_parent // local_beams
    target = source * capacity + arrival_ranks(source)
    slot_total = device_count * capacity
    all_parents = parent_beam.reshape(device_count, local_beams)
    all_sources = all_parents // local_beams
    destination = jnp.broadcast_to(
        jnp.arange(device_count, dtype=jnp.int32)[:, None], (device_count, local_beams)
    )
    placed = jnp.where(
        all_sources == device_rank, destination * capacity + arrival_ranks(all_sources), slot_total
    )
    outgoing = (
        jnp.zeros((slot_total,), jnp.int32)
        .at[placed.reshape(-1)]
        .set((all_parents % local_beams).reshape(-1), mode="drop")
    )
    packed = jnp.take(key_value_cache, outgoing, axis=0)
    arrived = lax.all_to_all(
        packed.reshape((device_count, capacity) + key_value_cache.shape[1:]),
        "dp",
        split_axis=0,
        concat_axis=0,
        tiled=True,
    )
    inherited = jnp.take(arrived.reshape((slot_total,) + key_value_cache.shape[1:]), target, axis=0)
    attention = attend(
        queries, inherited[:, :, 0], inherited[:, :, 1], key_new, value_new, position
    )
    attention = jnp.where(my_alive[:, None] > 0, attention, jnp.zeros_like(attention))
    partial_sum = jnp.dot(
        lax.all_gather(attention, "dp", axis=0, tiled=True),
        output_weight,
        preferred_element_type=jnp.float32,
    )
    return lax.psum(partial_sum, "tensor").astype(jnp.bfloat16)


def solution(mesh):
    placed = (
        P("dp", None),
        P("dp"),
        P("dp", "tensor"),
        P("dp", "tensor"),
        P("dp", "tensor"),
        P("tensor", "dp"),
        P("dp", None, None, "tensor", None),
        P(),
        P(),
        P(),
    )
    return jax.shard_map(body, mesh=mesh, in_specs=placed, out_specs=P(None, "dp"), check_vma=False)
```

profile of v0, /device:TPU:0, one launch (start us, length us, event | category | flops | bytes accessed | tf_op | source)
XLA Modules:
  0.0 575.5 jit_solution(12360558922635103368)
XLA Ops:
  6.5 1.9 copy.63
  8.5 7.3 %all-to-all-start = ((bf16[32,8,1024]{2,0,1:T(8,128)(2,1)}), bf16[32,8,1024]{2,0,1:T(8,128)(2,1)S(1)}, u32[]{:S(2)}, u32[]{:S(2)}) async-start(bf16[32,8,1024]{2,0,1:T(8,128)(2,1)} %bitcast.64), calls=%async_computation | async-start | bytes 1048576 | tf_op jit(solution)/shard_map/all_to_all | solution.py:87
  15.8 0.8 reshape.217
  16.5 0.3 convert_reduce_fusion
  17.0 0.7 and_select_fusion
  17.7 1.4 scatter_custom_fusion
  19.2 38.0 %gather_fusion.1 = bf16[64,256,2,2,128]{4,3,2,1,0:T(2,128)(2,1)} fusion(bf16[32,256,2,2,128]{4,3,2,1,0:T(2,128)(2,1)} %param.16, s32[1024]{0:T(1024)S(1)} %pad_clamp_fusion.1), kind=kCustom, calls=%fused_computation.1 | custom fusion | bytes 33554688 | tf_op jit(solution)/shard_map/jit(_take)/gather | solution.py:145
  57.3 15.2 %copy_select_fusion = bf16[8,8,256,2,2,128]{5,2,4,3,1,0:T(8,128)(2,1)} fusion(bf16[8,8,256,2,2,128]{5,4,3,2,1,0:T(2,128)(2,1)} %bitcast.65, pred[8,8]{1,0:T(8,128)(4,1)S(1)} %broadcast_in_dim.109), kind=kLoop, calls=%fused_computation.4 | loop fusion | flops 8388608 | bytes 33554496 | tf_op jit(solution)/shard_map/jit(_take)/select_n | solution.py:145
  72.4 6.0 %all-to-all-start.1 = ((bf16[8,8,256,2,2,128]{5,2,4,3,1,0:T(8,128)(2,1)}), bf16[8,8,256,2,2,128]{5,2,4,3,1,0:T(8,128)(2,1)}, u32[]{:S(2)}, u32[]{:S(2)}) async-start(bf16[8,8,256,2,2,128]{5,2,4,3,1,0:T(8,128)(2,1)} %copy_select_fusion), calls=%async_computation.2 | async-start | bytes 33554432 | tf_op jit(solution)/shard_map/all_to_all | solution.py:146
  78.6 0.3 fusion.28
  79.0 0.3 fusion.27
  79.3 3.5 fusion.26
  82.8 1.7 pad_maximum_fusion
  84.5 0.2 all-gather.2.cloned.1.call-start
  84.9 0.7 gather_fusion
  85.7 0.2 convert_reduce_fusion.1
  85.9 0.2 multiply_reduce_fusion
  86.2 0.1 multiply_cosine_fusion
  86.3 371.0 %reduce-scatter.2.cloned.1.call-done = f32[32,2560]{1,0:T(8,128)} async-done(((f32[256,2560]{1,0:T(8,128)}), f32[32,2560]{1,0:T(8,128)}) %reduce-scatter.2.cloned.1.call-update) | async-done | bytes 327696 | tf_op jit(solution)/shard_map/reduce_scatter | solution.py:94
  457.3 1.1 broadcast_multiply_fusion
  458.7 0.2 fusion.10
  458.9 0.3 fusion.12
  459.3 13.7 %all-to-all-done.1 = bf16[8,8,256,2,2,128]{5,2,4,3,1,0:T(8,128)(2,1)} async-done(((bf16[8,8,256,2,2,128]{5,2,4,3,1,0:T(8,128)(2,1)}), bf16[8,8,256,2,2,128]{5,2,4,3,1,0:T(8,128)(2,1)}, u32[]{:S(2)}, u32[]{:S(2)}) %all-to-all-start.1) | async-done | bytes 16777248 | tf_op jit(solution)/shard_map/all_to_all | solution.py:146
  473.0 10.8 %gather_fusion.2 = bf16[32,256,2,2,128]{4,1,3,2,0:T(8,128)(2,1)} fusion(bf16[64,256,2,2,128]{4,1,3,2,0:T(8,128)(2,1)} %bitcast.5, s32[1024]{0:T(1024)S(1)} %pad_clamp_fusion), kind=kCustom, calls=%fused_computation.2 | custom fusion | bytes 16777344 | tf_op jit(solution)/shard_map/jit(_take)/gather | solution.py:153
  483.8 7.5 %copy_select_fusion.1 = bf16[32,256,2,2,128]{4,1,3,0,2:T(8,128)(2,1)} fusion(bf16[32,256,2,2,128]{4,1,3,2,0:T(8,128)(2,1)} %gather_fusion.2, pred[32]{0:T(512)(128)(4,1)S(1)} %get-tuple-element.7), kind=kLoop, calls=%fused_computation.5 | loop fusion | flops 4194304 | bytes 16777248 | tf_op jit(solution)/shard_map/jit(_take)/select_n | solution.py:153
  491.3 3.5 fusion.25
  495.0 0.3 fusion.7
  495.6 2.9 fusion.5
  498.5 0.7 bitcast_select_fusion
  499.3 40.0 %all-gather.2.cloned.1.call-done = bf16[256,2048]{1,0:T(8,128)(2,1)} async-done(((bf16[32,2048]{1,0:T(8,128)(2,1)}), bf16[256,2048]{1,0:T(8,128)(2,1)}) %all-gather.2.cloned.1.call-update) | async-done | bytes 1048592 | tf_op jit(solution)/shard_map/all_gather | solution.py:159
  539.3 3.8 fusion.29
  543.1 25.6 %all-reduce.1 = bf16[256,1024]{1,0:T(8,128)(2,1)} all-reduce(f32[256,1024]{1,0:T(8,128)S(1)} %fusion.29), channel_id=1, replica_groups=mesh['dp'=8,'tensor'=4] {'tensor'}, use_global_device_ids=true, to_apply=%region_7.8 | all-reduce | flops 262144 | bytes 1572864 | tf_op jit(solution)/shard_map/psum | solution.py:163
  (54 shorter events, 1.6 us)
Async XLA Ops:
  6.5 72.1 %copy-start = (bf16[1024,256]{1,0:T(8,128)(2,1)S(1)}, bf16[1024,256]{1,0:T(8,128)(2,1)}, u32[]{:S(2)}) copy-start(bf16[1024,256]{1,0:T(8,128)(2,1)} %param.14) | copy-start | bytes 1572868
  8.5 64.0 %all-to-all-start = ((bf16[32,8,1024]{2,0,1:T(8,128)(2,1)}), bf16[32,8,1024]{2,0,1:T(8,128)(2,1)S(1)}, u32[]{:S(2)}, u32[]{:S(2)}) async-start(bf16[32,8,1024]{2,0,1:T(8,128)(2,1)} %bitcast.64), calls=%async_computation | async-start | bytes 1048576 | tf_op jit(solution)/shard_map/all_to_all | solution.py:87
  72.4 6.0 %copy-start.5 = (bf16[1024]{0:T(1024)(128)(2,1)S(1)}, bf16[1024]{0:T(1024)(128)(2,1)}, u32[]{:S(2)}) copy-start(bf16[1024]{0:T(1024)(128)(2,1)} %param.11) | copy-start | bytes 6148
  72.4 6.5 %copy-start.3 = (bf16[1024,256]{1,0:T(8,128)(2,1)S(1)}, bf16[1024,256]{1,0:T(8,128)(2,1)}, u32[]{:S(2)}) copy-start(bf16[1024,256]{1,0:T(8,128)(2,1)} %param.13) | copy-start | bytes 1572868
  72.4 400.6 %all-to-all-start.1 = ((bf16[8,8,256,2,2,128]{5,2,4,3,1,0:T(8,128)(2,1)}), bf16[8,8,256,2,2,128]{5,2,4,3,1,0:T(8,128)(2,1)}, u32[]{:S(2)}, u32[]{:S(2)}) async-start(bf16[8,8,256,2,2,128]{5,2,4,3,1,0:T(8,128)(2,1)} %copy_select_fusion), calls=%async_computation.2 | async-start | bytes 33554432 | tf_op jit(solution)/shard_map/all_to_all | solution.py:146
  78.4 378.9 %reduce-scatter.2.cloned.1.call-start = ((), (), s32[]{:S(2)}) async-start(), calls=%async_computation.3 | async-start | bytes 2949120 | tf_op jit(solution)/shard_map/reduce_scatter | solution.py:94
  78.9 5.8 %copy-start.4 = (s32[256]{0:T(256)S(1)}, s32[256]{0:T(256)}, u32[]{:S(2)}) copy-start(s32[256]{0:T(256)} %param.18) | copy-start | bytes 3076
  79.0 5.9 %copy-start.1 = (s32[256]{0:T(256)S(1)}, s32[256]{0:T(256)}, u32[]{:S(2)}) copy-start(s32[256]{0:T(256)} %param.17) | copy-start | bytes 3076
  79.0 6.6 %copy-start.6 = (s32[256]{0:T(256)S(1)}, s32[256]{0:T(256)}, u32[]{:S(2)}) copy-start(s32[256]{0:T(256)} %param.19) | copy-start | bytes 3076
  79.0 6.9 %copy-start.2 = (bf16[32,8192]{1,0:T(8,128)(2,1)S(1)}, bf16[32,8192]{1,0:T(8,128)(2,1)}, u32[]{:S(2)}) copy-start(bf16[32,8192]{1,0:T(8,128)(2,1)} %param.10) | copy-start | bytes 1572868
  84.5 454.8 %all-gather.2.cloned.1.call-start = ((), (), s32[]{:S(2)}) async-start(), calls=%async_computation.4 | async-start | bytes 1179648 | tf_op jit(solution)/shard_map/all_gather | solution.py:159
Sparse Core Ops, SparseCore 0:
  84.6 372.6 reduce-scatter.1
  499.4 39.8 all-gather.1
where the time goes:
time: 576 us; the launch traced here: 575 us
  waiting for transfers between devices  425 us (74%)
  local copies, waits for them, and re-layouts  54.4 us (9%)
  other arithmetic  29 us (5%)
  blocking collectives  25.6 us (4%)
  matrix products  14.5 us (3%)
  between operations  13.7 us (2%)
  starting transfers between devices  13.5 us (2%)
    reduce_scatter x1, waiting for transfers between devices, body(): lax.psum_scatter(jnp.concatenate([jnp.dot(scaled, query_weight, preferred...  371 us
    all_gather x1, waiting for transfers between devices, body(): lax.all_gather(attention, 'dp', axis=0, tiled=True)  40 us
    gather x1, local copies, waits for them, and re-layouts, body(): packed = jnp.take(key_value_cache, outgoing, axis=0)  38 us
    psum x1, blocking collectives, body(): return lax.psum(partial_sum, 'tensor').astype(jnp.bfloat16)  25.6 us
    select_n x2, other arithmetic, body(): packed = jnp.take(key_value_cache, outgoing, axis=0)  15.2 us
    all_to_all x1, waiting for transfers between devices, body(): lax.all_to_all(packed.reshape((device_count, capacity) + key_value_cache....  13.7 us
  transfers between devices with their start and end apart: 4, of which 3 were waited for; matrix products, arithmetic and copies ran while one was open for 11% of the time, Pallas kernels for 0%

commit v1 on v0

v1 whole, which is shorter than its diff:
```python
import functools
import math

import jax
import jax.numpy as jnp
from jax import lax
from jax.experimental import pallas as pl
from jax.experimental.pallas import tpu as pltpu
from jax.sharding import PartitionSpec as P

HEAD_DIM = 128


def rotate(vectors, position):
    half_width = vectors.shape[-1] // 2
    pair_index = jnp.arange(half_width).astype(jnp.float32)
    frequency = jnp.exp(pair_index * (-2.0 * math.log(1000000.0) / vectors.shape[-1]))
    angles = position.astype(jnp.float32)[:, None] * frequency[None, :]
    cosine = jnp.cos(angles)[:, None, :]
    sine_part = jnp.sin(angles)[:, None, :]
    first_half = vectors[..., :half_width]
    second = vectors[..., half_width:]
    return jnp.concatenate(
        [first_half * cosine - second * sine_part, second * cosine + first_half * sine_part],
        axis=-1,
    )


def attend_kernel(capacity, head_count, parent_ref, length_ref, new_ref, cache_ref, out_ref):
    groups = cache_ref.shape[2]
    length = cache_ref.shape[3]
    per_group = head_count // groups
    first = pl.program_id(0) * capacity
    score_scale = 1.0 / math.sqrt(HEAD_DIM)
    rows = groups * per_group
    scores, latest, limits = [], [], []
    for slot in range(capacity):
        parent = parent_ref[first + slot]
        limits.append(jnp.full((rows, 1), length_ref[first + slot], jnp.int32))
        for group in range(groups):
            query = new_ref[0, slot, group * per_group : (group + 1) * per_group, :]
            key_row = new_ref[0, slot, head_count + group : head_count + group + 1, :]
            keys = cache_ref[parent, 0, group]
            scores.append(
                lax.dot_general(
                    query, keys, (((1,), (1,)), ((), ())), preferred_element_type=jnp.float32
                )
            )
            latest.append(
                jnp.sum(
                    query.astype(jnp.float32) * key_row.astype(jnp.float32), axis=1, keepdims=True
                )
            )
    cached = jnp.concatenate(scores, axis=0) * score_scale
    newest = jnp.concatenate(latest, axis=0) * score_scale
    limit = jnp.concatenate(limits, axis=0)
    slots = lax.broadcasted_iota(jnp.int32, cached.shape, 1)
    cached = jnp.where(slots < limit, cached, -jnp.inf)
    highest = jnp.maximum(jnp.max(cached, axis=1, keepdims=True), newest)
    cached_exp = jnp.exp(cached - highest)
    newest_exp = jnp.exp(newest - highest)
    denominator = jnp.sum(cached_exp, axis=1, keepdims=True) + newest_exp
    weight = (cached_exp / denominator).astype(jnp.bfloat16)
    newest_weight = (newest_exp / denominator).astype(jnp.bfloat16).astype(jnp.float32)
    for slot in range(capacity):
        parent = parent_ref[first + slot]
        parts = []
        for group in range(groups):
            low = (slot * groups + group) * per_group
            values = cache_ref[parent, 1, group]
            value_row = new_ref[
                0, slot, head_count + groups + group : head_count + groups + group + 1, :
            ]
            mixed = jnp.dot(
                weight[low : low + per_group], values, preferred_element_type=jnp.float32
            )
            mixed = mixed + newest_weight[low : low + per_group] * value_row.astype(jnp.float32)
            parts.append(mixed)
        out_ref[0, slot] = jnp.concatenate(parts, axis=0).astype(jnp.bfloat16)


def attend(parents, lengths, arrived, cache, head_count):
    device_count, capacity, rows, _ = arrived.shape
    whole = cache.shape
    spec = pltpu.PrefetchScalarGridSpec(
        num_scalar_prefetch=2,
        grid=(device_count,),
        in_specs=[
            pl.BlockSpec((1, capacity, rows, HEAD_DIM), lambda i, *_: (i, 0, 0, 0)),
            pl.BlockSpec(whole, lambda i, *_: (0, 0, 0, 0, 0)),
        ],
        out_specs=pl.BlockSpec((1, capacity, head_count, HEAD_DIM), lambda i, *_: (i, 0, 0, 0)),
    )
    return pl.pallas_call(
        functools.partial(attend_kernel, capacity, head_count),
        grid_spec=spec,
        out_shape=jax.ShapeDtypeStruct(
            (device_count, capacity, head_count, HEAD_DIM), jnp.bfloat16
        ),
        compiler_params=pltpu.CompilerParams(vmem_limit_bytes=40 * 1024 * 1024),
        name="attend",
    )(parents, lengths, arrived, cache)


def arrival_ranks(sources):
    ordinal = jnp.arange(sources.shape[-1], dtype=jnp.int32)
    earlier = (sources[..., None, :] == sources[..., :, None]) & (
        ordinal[None, :] < ordinal[:, None]
    )
    return jnp.sum(earlier.astype(jnp.int32), axis=-1)


def body(
    hidden_in,
    norm_gain,
    query_weight,
    key_weight,
    value_weight,
    output_weight,
    key_value_cache,
    cache_lengths,
    parent_beam,
    beam_alive,
):
    device_count = lax.axis_size("dp")
    device_rank = lax.axis_index("dp")
    local_beams = hidden_in.shape[0]
    capacity = max(2, (2 * local_beams + device_count - 1) // device_count)
    slot_total = device_count * capacity
    query_width = query_weight.shape[1]
    key_width = key_weight.shape[1]
    head_count = query_width // HEAD_DIM
    group_count = key_width // HEAD_DIM
    row_count = head_count + 2 * group_count

    cache = jnp.transpose(key_value_cache, (0, 2, 3, 1, 4))

    all_parents = parent_beam.reshape(device_count, local_beams)
    all_sources = all_parents // local_beams
    all_ranks = arrival_ranks(all_sources)
    beam_index = jnp.arange(parent_beam.shape[0], dtype=jnp.int32)
    all_positions = jnp.sum(
        jnp.where(parent_beam[:, None] == beam_index[None, :], cache_lengths[None, :], 0), axis=1
    )
    held = (all_sources == device_rank)[:, None, :] & (
        all_ranks[:, None, :] == jnp.arange(capacity, dtype=jnp.int32)[None, :, None]
    )
    slot_parent = jnp.sum(jnp.where(held, (all_parents % local_beams)[:, None, :], 0), axis=2)
    slot_length = jnp.sum(
        jnp.where(held, all_positions.reshape(device_count, 1, local_beams), 0), axis=2
    )

    first_beam = device_rank * local_beams
    my_alive = lax.dynamic_slice_in_dim(beam_alive, first_beam, local_beams)
    position = lax.dynamic_slice_in_dim(all_positions, first_beam, local_beams)
    my_source = lax.dynamic_slice_in_dim(all_sources, device_rank, 1)[0]
    my_rank = lax.dynamic_slice_in_dim(all_ranks, device_rank, 1)[0]
    target = my_source * capacity + my_rank
    placing = (jnp.arange(slot_total, dtype=jnp.int32)[:, None] == target[None, :]).astype(
        jnp.bfloat16
    )
    picking = (
        (jnp.arange(slot_total, dtype=jnp.int32)[None, :] == target[:, None])
        & (my_alive[:, None] > 0)
    ).astype(jnp.bfloat16)

    hidden_float = hidden_in.astype(jnp.float32)
    inverse = lax.rsqrt(jnp.mean(hidden_float * hidden_float, axis=1) + 1e-06)
    blocked = lax.all_to_all(hidden_in, "dp", split_axis=1, concat_axis=0, tiled=True)
    scaled = (blocked.astype(jnp.float32) * norm_gain.astype(jnp.float32)[None, :]).astype(
        jnp.bfloat16
    )
    partial = jnp.concatenate(
        [
            jnp.dot(scaled, weight, preferred_element_type=jnp.float32).astype(jnp.bfloat16)
            for weight in (query_weight, key_weight, value_weight)
        ],
        axis=1,
    ).reshape(device_count, local_beams, query_width + 2 * key_width)
    partial = lax.all_to_all(partial, "dp", split_axis=0, concat_axis=0, tiled=True)
    summed = jnp.sum(partial.astype(jnp.float32), axis=0) * inverse[:, None]
    heads = summed.reshape(local_beams, row_count, HEAD_DIM)
    turned = rotate(heads[:, : head_count + group_count], position)
    fresh = jnp.concatenate([turned, heads[:, head_count + group_count :]], axis=1).astype(
        jnp.bfloat16
    )
    packed = jnp.dot(
        placing, fresh.reshape(local_beams, row_count * HEAD_DIM), preferred_element_type=jnp.float32
    ).astype(jnp.bfloat16)
    arrived = lax.all_to_all(
        packed.reshape(device_count, capacity, row_count, HEAD_DIM),
        "dp",
        split_axis=0,
        concat_axis=0,
        tiled=True,
    )
    mixed = attend(
        slot_parent.reshape(-1), slot_length.reshape(-1), arrived, cache, head_count
    )
    back = lax.all_to_all(mixed, "dp", split_axis=0, concat_axis=0, tiled=True)
    attention = jnp.dot(
        picking, back.reshape(slot_total, query_width), preferred_element_type=jnp.float32
    ).astype(jnp.bfloat16)
    gathered = lax.all_to_all(
        jnp.broadcast_to(attention[None], (device_count,) + attention.shape),
        "dp",
        split_axis=0,
        concat_axis=0,
        tiled=True,
    ).reshape(device_count * local_beams, query_width)
    partial_sum = jnp.dot(gathered, output_weight, preferred_element_type=jnp.float32)
    return lax.psum(partial_sum, "tensor").astype(jnp.bfloat16)


def solution(mesh):
    placed = (
        P("dp", None),
        P("dp"),
        P("dp", "tensor"),
        P("dp", "tensor"),
        P("dp", "tensor"),
        P("tensor", "dp"),
        P("dp", None, None, "tensor", None),
        P(),
        P(),
        P(),
    )
    return jax.shard_map(body, mesh=mesh, in_specs=placed, out_specs=P(None, "dp"), check_vma=False)
```

time: 576 us -> 164 us (0.28)
  waiting for transfers between devices: 425 us -> 53.5 us
  local copies, waits for them, and re-layouts: 54.4 us -> 14.9 us
  blocking collectives: 25.6 us -> 54.3 us
  other arithmetic: 29 us -> 3.98 us
  between operations: 13.7 us -> 0.2 us
  Pallas kernels: 0 us -> 7.96 us
  starting transfers between devices: 13.5 us -> 19.7 us
  matrix products: 14.5 us -> 8.72 us
    reduce_scatter x1 -> x0, waiting for transfers between devices: 371 us -> none  [body(): lax.psum_scatter(jnp.concatenate([jnp.dot(scaled, query_weight, preferred...]
    gather x3 -> x0, local copies, waits for them, and re-layouts: 49.5 us -> none  [the longest x1 38 us: body(): packed = jnp.take(key_value_cache, outgoing, axis=0)]
    all_gather x1 -> x0, waiting for transfers between devices: 40 us -> none  [body(): lax.all_gather(attention, 'dp', axis=0, tiled=True)]
    all_to_all x0 -> x1, blocking collectives: none -> 28.7 us  [body(): lax.all_to_all(jnp.broadcast_to(attention[None], (device_count,) + attent...]
    all_to_all x1 -> x3, waiting for transfers between devices: 13.7 us -> 39.7 us  [the longest x1 30.5 us: body(): lax.all_to_all(partial, 'dp', split_axis=0, concat_axis=0, tiled=True)]
    select_n x6 -> x0, other arithmetic: 23.5 us -> none  [the longest x2 15.2 us: body(): packed = jnp.take(key_value_cache, outgoing, axis=0)]
    all_to_all x1, waiting for transfers between devices: 0.01 us -> 13.8 us  [body(): lax.all_to_all(hidden_in, 'dp', split_axis=1, concat_axis=0, tiled=True)]
    unnamed x16 -> x15, local copies, waits for them, and re-layouts: 0.11 us -> 12.4 us
  transfers between devices with their start and end apart: 4 -> 4, of which waited for: 3 -> 4; matrix products, arithmetic and copies ran while one was open for 11% -> 7% of each run, Pallas kernels for 0% -> 0%
where the time goes in v1:
time: 164 us; the launch traced here: 163 us
  blocking collectives  54.3 us (33%)
  waiting for transfers between devices  53.5 us (33%)
  starting transfers between devices  19.7 us (12%)
  local copies, waits for them, and re-layouts  14.9 us (9%)
  matrix products  8.72 us (5%)
  Pallas kernels  7.96 us (5%)
  other arithmetic  3.98 us (2%)
    all_to_all x1, waiting for transfers between devices, body(): lax.all_to_all(partial, 'dp', split_axis=0, concat_axis=0, tiled=True)  30.5 us
    all_to_all x1, blocking collectives, body(): lax.all_to_all(jnp.broadcast_to(attention[None], (device_count,) + attent...  28.7 us
    psum x1, blocking collectives, body(): return lax.psum(partial_sum, 'tensor').astype(jnp.bfloat16)  25.6 us
    all_to_all x1, waiting for transfers between devices, body(): lax.all_to_all(hidden_in, 'dp', split_axis=1, concat_axis=0, tiled=True)  13.8 us
    unnamed x15, local copies, waits for them, and re-layouts  12.4 us
    all_to_all x1, waiting for transfers between devices, body(): back = lax.all_to_all(mixed, 'dp', split_axis=0, concat_axis=0, tiled=True)  8.44 us
    pallas_call x1, Pallas kernels, attend(): pl.pallas_call(functools.partial(attend_kernel, capacity, head_count), gr...  7.96 us
    all_to_all x1, starting transfers between devices, body(): lax.all_to_all(hidden_in, 'dp', split_axis=1, concat_axis=0, tiled=True)  7.28 us
  transfers between devices with their start and end apart: 4, of which 4 were waited for; matrix products, arithmetic and copies ran while one was open for 7% of the time, Pallas kernels for 0%

profile of v1, /device:TPU:0, one launch (start us, length us, event | category | flops | bytes accessed | tf_op | source)
XLA Modules:
  0.0 163.4 jit_solution(10877212576526636095)
XLA Ops:
  0.0 2.0 %copy.49 = bf16[4,8,8,1024]{3,2,0,1:T(8,128)(2,1)} copy(bf16[4,8,8,1024]{3,2,1,0:T(8,128)(2,1)} %bitcast.37) | data formatting | bytes 1048576 | tf_op jit(solution)/shard_map/all_to_all | solution.py:169
  2.0 7.3 %all-to-all-start = ((bf16[32,8,1024]{2,0,1:T(8,128)(2,1)}), bf16[32,8,1024]{2,0,1:T(8,128)(2,1)S(1)}, u32[]{:S(2)}, u32[]{:S(2)}) async-start(bf16[32,8,1024]{2,0,1:T(8,128)(2,1)} %bitcast.35), calls=%async_computation | async-start | bytes 1048576 | tf_op jit(solution)/shard_map/all_to_all | solution.py:169
  9.3 0.7 convert_element_type.63
  9.9 13.8 %all-to-all-done = bf16[32,8,1024]{2,0,1:T(8,128)(2,1)S(1)} async-done(((bf16[32,8,1024]{2,0,1:T(8,128)(2,1)}), bf16[32,8,1024]{2,0,1:T(8,128)(2,1)S(1)}, u32[]{:S(2)}, u32[]{:S(2)}) %all-to-all-start) | async-done | bytes 524320 | tf_op jit(solution)/shard_map/all_to_all | solution.py:169
  23.7 0.1 fusion.1
  23.9 0.3 convolution_convert_fusion.3
  24.2 0.3 convolution_convert_fusion.4
  24.5 3.5 %convolution_convert_fusion.1 = bf16[256,2048]{1,0:T(8,128)(2,1)S(1)} fusion(bf16[256,1024]{1,0:T(8,128)(2,1)S(1)} %fusion.1, bf16[1024,2048]{1,0:T(8,128)(2,1)} %param.12), kind=kOutput, calls=%fused_computation.3 | convolution fusion | flops 1074266112 | bytes 5767168 | tf_op jit(solution)/shard_map/dot_general | solution.py:175
  28.0 1.2 pad_maximum_fusion
  29.2 3.6 %all-to-all-start.1 = ((bf16[8,32,2560]{2,1,0:T(8,128)(2,1)}), bf16[8,32,2560]{2,1,0:T(8,128)(2,1)S(1)}, u32[]{:S(2)}, u32[]{:S(2)}) async-start(bf16[8,32,2560]{2,1,0:T(8,128)(2,1)} %bitcast.3), calls=%async_computation.1 | async-start | bytes 2621440 | tf_op jit(solution)/shard_map/all_to_all | solution.py:180
  32.9 0.2 select_reduce_fusion
  33.2 0.3 convert_reduce_fusion.1
  33.5 0.2 multiply_reduce_fusion
  33.8 0.1 multiply_cosine_fusion
  33.9 30.5 %all-to-all-done.1 = bf16[8,32,2560]{2,1,0:T(8,128)(2,1)S(1)} async-done(((bf16[8,32,2560]{2,1,0:T(8,128)(2,1)}), bf16[8,32,2560]{2,1,0:T(8,128)(2,1)S(1)}, u32[]{:S(2)}, u32[]{:S(2)}) %all-to-all-start.1) | async-done | bytes 1310752 | tf_op jit(solution)/shard_map/all_to_all | solution.py:180
  64.4 0.2 convert_reduce_fusion
  64.7 0.2 subtract_convert_fusion
  64.9 0.1 pad_maximum_fusion.1
  65.1 1.0 fusion
  66.0 3.6 %all-to-all-start.2 = ((bf16[8,8,20,128]{3,1,2,0:T(8,128)(2,1)}), bf16[8,8,20,128]{3,1,2,0:T(8,128)(2,1)S(1)}, u32[]{:S(2)}, u32[]{:S(2)}) async-start(bf16[8,8,20,128]{3,1,2,0:T(8,128)(2,1)} %fusion), calls=%async_computation.2 | async-start | bytes 655360 | tf_op jit(solution)/shard_map/all_to_all | solution.py:190
  69.8 0.3 select_reduce_fusion.1
  70.3 9.0 %copy.48 = bf16[32,256,2,2,128]{4,1,3,2,0:T(8,128)(2,1)} copy(bf16[32,256,2,2,128]{4,3,2,1,0:T(2,128)(2,1)} %param.16) | data formatting | bytes 16777216 | tf_op args[6]
  79.3 0.8 all-to-all-done.2
  80.2 3.4 %copy-done.1 = bf16[32,256,2,2,128]{4,1,3,2,0:T(8,128)(2,1)S(1)} copy-done((bf16[32,256,2,2,128]{4,1,3,2,0:T(8,128)(2,1)S(1)}, bf16[32,256,2,2,128]{4,1,3,2,0:T(8,128)(2,1)}, u32[]{:S(2)}) %copy-start.1) | copy-done | bytes 8388632
  83.6 8.0 %attend.1 = bf16[8,8,16,128]{3,2,1,0:T(8,128)(2,1)} custom-call(s32[64]{0:T(128)S(1)} %reshape.214.parent_ref, s32[64]{0:T(128)S(1)} %reshape.215.length_ref, bf16[8,8,20,128]{3,2,1,0:T(8,128)(2,1)S(1)} %copy.32.new_ref, bf16[32,2,2,256,128]{4,3,2,1,0:T(8,128)(2,1)S(1)} %bitcast.36), custom_call_target="tpu_custom_call" | custom-call | tf_op jit(solution)/shard_map/attend/pallas_call | solution.py:94
  91.5 5.2 %all-to-all-start.3 = ((bf16[8,8,16,128]{3,2,1,0:T(8,128)(2,1)}), bf16[8,8,16,128]{3,2,1,0:T(8,128)(2,1)S(1)}, u32[]{:S(2)}, u32[]{:S(2)}) async-start(bf16[8,8,16,128]{3,2,1,0:T(8,128)(2,1)} %attend.1), calls=%async_computation.3 | async-start | bytes 524288 | tf_op jit(solution)/shard_map/all_to_all | solution.py:200
  96.8 8.4 %all-to-all-done.3 = bf16[8,8,16,128]{3,2,1,0:T(8,128)(2,1)S(1)} async-done(((bf16[8,8,16,128]{3,2,1,0:T(8,128)(2,1)}), bf16[8,8,16,128]{3,2,1,0:T(8,128)(2,1)S(1)}, u32[]{:S(2)}, u32[]{:S(2)}) %all-to-all-start.3) | async-done | bytes 262176 | tf_op jit(solution)/shard_map/all_to_all | solution.py:200
  105.2 0.2 convolution_convert_fusion.2
  105.5 0.1 broadcast_in_dim.40
  105.6 28.7 %all_to_all.33 = bf16[8,32,2048]{2,1,0:T(8,128)(2,1)S(1)} all-to-all(bf16[8,32,2048]{2,1,0:T(8,128)(2,1)S(1)} %broadcast_in_dim.40), channel_id=1, replica_groups=mesh['dp'=8,'tensor'=4] {'dp'}, dimensions={0} | all-to-all | bytes 2097152 | tf_op jit(solution)/shard_map/all_to_all | solution.py:204
  134.3 3.5 %fusion.14 = f32[256,1024]{1,0:T(8,128)S(1)} fusion(bf16[256,2048]{1,0:T(8,128)(2,1)S(1)} %bitcast.38, bf16[2048,1024]{1,0:T(8,128)(2,1)} %param.15), kind=kOutput, calls=%fused_computation.52 | convolution fusion | flops 1073741824 | bytes 6291456 | tf_op jit(solution)/shard_map/dot_general | solution.py:211
  137.8 25.6 %all-reduce.1 = bf16[256,1024]{1,0:T(8,128)(2,1)} all-reduce(f32[256,1024]{1,0:T(8,128)S(1)} %fusion.14), channel_id=1, replica_groups=mesh['dp'=8,'tensor'=4] {'tensor'}, use_global_device_ids=true, to_apply=%region_6.7 | all-reduce | flops 262144 | bytes 1572864 | tf_op jit(solution)/shard_map/psum | solution.py:212
  (29 shorter events, 0.8 us)
Async XLA Ops:
  0.0 23.8 %copy-start = (bf16[1024,256]{1,0:T(8,128)(2,1)S(1)}, bf16[1024,256]{1,0:T(8,128)(2,1)}, u32[]{:S(2)}) copy-start(bf16[1024,256]{1,0:T(8,128)(2,1)} %param.14) | copy-start | bytes 1572868
  0.0 24.2 %copy-start.3 = (bf16[1024,256]{1,0:T(8,128)(2,1)S(1)}, bf16[1024,256]{1,0:T(8,128)(2,1)}, u32[]{:S(2)}) copy-start(bf16[1024,256]{1,0:T(8,128)(2,1)} %param.13) | copy-start | bytes 1572868
  2.0 21.8 %all-to-all-start = ((bf16[32,8,1024]{2,0,1:T(8,128)(2,1)}), bf16[32,8,1024]{2,0,1:T(8,128)(2,1)S(1)}, u32[]{:S(2)}, u32[]{:S(2)}) async-start(bf16[32,8,1024]{2,0,1:T(8,128)(2,1)} %bitcast.35), calls=%async_computation | async-start | bytes 1048576 | tf_op jit(solution)/shard_map/all_to_all | solution.py:169
  28.0 4.8 %copy-start.4 = (s32[256]{0:T(256)S(1)}, s32[256]{0:T(256)}, u32[]{:S(2)}) copy-start(s32[256]{0:T(256)} %param.18) | copy-start | bytes 3076
  28.0 4.9 %copy-start.5 = (s32[256]{0:T(256)S(1)}, s32[256]{0:T(256)}, u32[]{:S(2)}) copy-start(s32[256]{0:T(256)} %param.17) | copy-start | bytes 3076
  28.0 5.5 %copy-start.2 = (bf16[32,8192]{1,0:T(8,128)(2,1)S(1)}, bf16[32,8192]{1,0:T(8,128)(2,1)}, u32[]{:S(2)}) copy-start(bf16[32,8192]{1,0:T(8,128)(2,1)} %param.10) | copy-start | bytes 1572868
  29.2 35.2 %all-to-all-start.1 = ((bf16[8,32,2560]{2,1,0:T(8,128)(2,1)}), bf16[8,32,2560]{2,1,0:T(8,128)(2,1)S(1)}, u32[]{:S(2)}, u32[]{:S(2)}) async-start(bf16[8,32,2560]{2,1,0:T(8,128)(2,1)} %bitcast.3), calls=%async_computation.1 | async-start | bytes 2621440 | tf_op jit(solution)/shard_map/all_to_all | solution.py:180
  66.0 14.1 %all-to-all-start.2 = ((bf16[8,8,20,128]{3,1,2,0:T(8,128)(2,1)}), bf16[8,8,20,128]{3,1,2,0:T(8,128)(2,1)S(1)}, u32[]{:S(2)}, u32[]{:S(2)}) async-start(bf16[8,8,20,128]{3,1,2,0:T(8,128)(2,1)} %fusion), calls=%async_computation.2 | async-start | bytes 655360 | tf_op jit(solution)/shard_map/all_to_all | solution.py:190
  80.2 3.4 %copy-start.1 = (bf16[32,256,2,2,128]{4,1,3,2,0:T(8,128)(2,1)S(1)}, bf16[32,256,2,2,128]{4,1,3,2,0:T(8,128)(2,1)}, u32[]{:S(2)}) copy-start(bf16[32,256,2,2,128]{4,1,3,2,0:T(8,128)(2,1)} %copy.48) | copy-start | bytes 25165828
  83.6 13.1 %copy-start.6 = (s32[256]{0:T(256)S(1)}, s32[256]{0:T(256)}, u32[]{:S(2)}) copy-start(s32[256]{0:T(256)} %param.19) | copy-start | bytes 3076
  91.5 13.7 %all-to-all-start.3 = ((bf16[8,8,16,128]{3,2,1,0:T(8,128)(2,1)}), bf16[8,8,16,128]{3,2,1,0:T(8,128)(2,1)S(1)}, u32[]{:S(2)}, u32[]{:S(2)}) async-start(bf16[8,8,16,128]{3,2,1,0:T(8,128)(2,1)} %attend.1), calls=%async_computation.3 | async-start | bytes 524288 | tf_op jit(solution)/shard_map/all_to_all | solution.py:200

commit v2 on v1

--- a/solution.py
+++ b/solution.py
@@ -11,18 +11,15 @@
 HEAD_DIM = 128
 
 
-def rotate(vectors, position):
-    half_width = vectors.shape[-1] // 2
+def turn_angles(position):
+    half_width = HEAD_DIM // 2
     pair_index = jnp.arange(half_width).astype(jnp.float32)
-    frequency = jnp.exp(pair_index * (-2.0 * math.log(1000000.0) / vectors.shape[-1]))
+    frequency = jnp.exp(pair_index * (-2.0 * math.log(1000000.0) / HEAD_DIM))
     angles = position.astype(jnp.float32)[:, None] * frequency[None, :]
-    cosine = jnp.cos(angles)[:, None, :]
-    sine_part = jnp.sin(angles)[:, None, :]
-    first_half = vectors[..., :half_width]
-    second = vectors[..., half_width:]
-    return jnp.concatenate(
-        [first_half * cosine - second * sine_part, second * cosine + first_half * sine_part],
-        axis=-1,
+    cosine, sine = jnp.cos(angles), jnp.sin(angles)
+    return (
+        jnp.concatenate([cosine, cosine], axis=1),
+        jnp.concatenate([-sine, sine], axis=1),
     )
 
 
@@ -102,6 +99,348 @@
     )(parents, lengths, arrived, cache)
 
 
+MESH = pl.DeviceIdType.MESH
+
+
+def remote(src, dst, send_sem, recv_sem, device):
+    return pltpu.make_async_remote_copy(
+        src_ref=src,
+        dst_ref=dst,
+        send_sem=send_sem,
+        recv_sem=recv_sem,
+        device_id=device,
+        device_id_type=MESH,
+    )
+
+
+def greet(devices):
+    barrier = pltpu.get_barrier_semaphore()
+    for device in devices:
+        pl.semaphore_signal(barrier, inc=1, device_id=device, device_id_type=MESH)
+    pl.semaphore_wait(barrier, len(devices))
+
+
+def scatter_sum(chunk, high, low, partner, peers, bufs):
+    product, half, got, block, landed, sems = bufs
+    half_send, half_recv, block_send, block_recv = sems
+    half[chunk] = product[chunk, :, 1 - low].astype(jnp.bfloat16)
+    first = remote(
+        half.at[chunk], got.at[chunk], half_send.at[chunk], half_recv.at[chunk], partner
+    )
+    first.start()
+
+    def second():
+        first.wait()
+        copies = []
+        for step, peer in enumerate(peers):
+            other = lax.rem(high + step + 1, len(peers) + 1)
+            block[chunk, step] = (
+                product[chunk, other, low] + got[chunk, other].astype(jnp.float32)
+            ).astype(jnp.bfloat16)
+            copy = remote(
+                block.at[chunk, step],
+                landed.at[chunk, step],
+                block_send.at[chunk, step],
+                block_recv.at[chunk, step],
+                peer,
+            )
+            copy.start()
+            copies.append(copy)
+
+        def finish():
+            for copy in copies:
+                copy.wait()
+            total = product[chunk, high, low] + got[chunk, high].astype(jnp.float32)
+            for step in range(len(peers)):
+                total = total + landed[chunk, step].astype(jnp.float32)
+            return total
+
+        return finish
+
+    return second
+
+
+def project_kernel(
+    n,
+    hidden_ref,
+    gain_ref,
+    query_ref,
+    key_ref,
+    value_ref,
+    cosine_ref,
+    sine_ref,
+    out_ref,
+    blocks,
+    product,
+    half,
+    got,
+    block,
+    landed,
+    move_send,
+    move_recv,
+    pass_send,
+    pass_recv,
+    half_send,
+    half_recv,
+    block_send,
+    block_recv,
+):
+    me = lax.axis_index("dp")
+    rank = lax.axis_index("tensor")
+    core = lax.rem(rank, 2)
+    twin = (me, rank + 1 - 2 * core)
+    high, low = me // 2, lax.rem(me, 2)
+    partner = (me + 1 - 2 * low, rank)
+    peers = [(lax.rem(high + d, n // 2) * 2 + low, rank) for d in range(1, n // 2)]
+    others = [(lax.rem(me + d, n), rank) for d in range(1, n)]
+    rows, depth = hidden_ref.shape[0], query_ref.shape[0]
+    part = rows // 2
+    greet(others + [twin])
+    mine = pl.ds(pl.multiple_of(core * part, part), part)
+    theirs = pl.ds(pl.multiple_of((1 - core) * part, part), part)
+    moves = []
+    for d in range(1, n):
+        target = lax.rem(me + d, n)
+        columns = pl.ds(pl.multiple_of(target * depth, depth), depth)
+        copy = remote(
+            hidden_ref.at[mine, columns],
+            blocks.at[d, mine],
+            move_send.at[d],
+            move_recv.at[d],
+            (target, rank),
+        )
+        copy.start()
+        moves.append(copy)
+    blocks[0] = hidden_ref[:, pl.ds(pl.multiple_of(me * depth, depth), depth)]
+    hidden = hidden_ref[...].astype(jnp.float32)
+    inverse = lax.rsqrt(
+        jnp.sum(hidden * hidden, axis=1, keepdims=True) / hidden_ref.shape[1] + 1e-06
+    )
+    passes = []
+    for d in range(1, n):
+        moves[d - 1].wait_recv()
+        copy = remote(
+            blocks.at[d, mine], blocks.at[d, mine], pass_send.at[d], pass_recv.at[d], twin
+        )
+        copy.start()
+        passes.append(copy)
+    for d in range(1, n):
+        moves[d - 1].wait_send()
+        passes[d - 1].wait_send()
+        remote(
+            blocks.at[d, theirs], blocks.at[d, theirs], pass_send.at[d], pass_recv.at[d], twin
+        ).wait_recv()
+    gain = gain_ref[...].astype(jnp.float32)
+    scaled = jnp.concatenate(
+        [(blocks[d].astype(jnp.float32) * gain).astype(jnp.bfloat16) for d in range(n)], axis=0
+    )
+    width = product.shape[-1]
+    chunks = product.shape[0]
+    bufs = (product, half, got, block, landed, (half_send, half_recv, block_send, block_recv))
+    seconds = []
+    for chunk in range(chunks):
+        if chunk < chunks - 1:
+            weight = query_ref[:, chunk * width : (chunk + 1) * width]
+        else:
+            weight = jnp.concatenate([key_ref[...], value_ref[...]], axis=1)
+        result = jnp.dot(scaled, weight, preferred_element_type=jnp.float32)
+        for d in range(n):
+            owner = lax.rem(me - d + n, n)
+            product[chunk, owner // 2, lax.rem(owner, 2)] = result[d * rows : (d + 1) * rows]
+        seconds.append(scatter_sum(chunk, high, low, partner, peers, bufs))
+    finishes = [second() for second in seconds]
+    cosine, sine = cosine_ref[...], sine_ref[...]
+    for chunk in range(chunks):
+        total = finishes[chunk]() * inverse
+        for first in range(0, width, HEAD_DIM):
+            vector = total[:, first : first + HEAD_DIM]
+            if chunk < chunks - 1 or first < width // 2:
+                vector = vector * cosine + pltpu.roll(vector, HEAD_DIM // 2, 1) * sine
+            at = chunk * width + first
+            out_ref[:, at : at + HEAD_DIM] = vector.astype(jnp.bfloat16)
+
+
+def sum_scratch(chunks, nh, rows, width):
+    return [
+        pltpu.VMEM((chunks, nh, 2, rows, width), jnp.float32),
+        pltpu.VMEM((chunks, nh, rows, width), jnp.bfloat16),
+        pltpu.VMEM((chunks, nh, rows, width), jnp.bfloat16),
+        pltpu.VMEM((chunks, max(nh - 1, 1), rows, width), jnp.bfloat16),
+        pltpu.VMEM((chunks, max(nh - 1, 1), rows, width), jnp.bfloat16),
+    ]
+
+
+def sum_sems(chunks, nh):
+    return [
+        pltpu.SemaphoreType.DMA((chunks,)),
+        pltpu.SemaphoreType.DMA((chunks,)),
+        pltpu.SemaphoreType.DMA((chunks, max(nh - 1, 1))),
+        pltpu.SemaphoreType.DMA((chunks, max(nh - 1, 1))),
+    ]
+
+
+def project(n, hidden, gain, query_weight, key_weight, value_weight, cosine, sine):
+    rows = hidden.shape[0]
+    depth, query_width = query_weight.shape
+    width = 2 * key_weight.shape[1]
+    chunks = query_width // width + 1
+    vmem = pl.BlockSpec(memory_space=pltpu.VMEM)
+    return pl.pallas_call(
+        functools.partial(project_kernel, n),
+        out_shape=jax.ShapeDtypeStruct((rows, chunks * width), jnp.bfloat16),
+        in_specs=[vmem] * 7,
+        out_specs=vmem,
+        scratch_shapes=[pltpu.VMEM((n, rows, depth), jnp.bfloat16)]
+        + sum_scratch(chunks, n // 2, rows, width)
+        + [pltpu.SemaphoreType.DMA((n,))] * 4
+        + sum_sems(chunks, n // 2),
+        compiler_params=pltpu.CompilerParams(
+            collective_id=0, has_side_effects=True, vmem_limit_bytes=40 * 1024 * 1024
+        ),
+        cost_estimate=pl.CostEstimate(
+            flops=2 * n * rows * depth * chunks * width, bytes_accessed=8000000, transcendentals=0
+        ),
+        name="project",
+    )(hidden, gain, query_weight, key_weight, value_weight, cosine, sine)
+
+
+def output_kernel(
+    n,
+    ranks,
+    mixed_ref,
+    weight_ref,
+    out_ref,
+    gathered,
+    whole,
+    product,
+    half,
+    got,
+    block,
+    landed,
+    own_send,
+    pass_send,
+    take_recv,
+    end_send,
+    end_pass,
+    end_recv,
+    half_send,
+    half_recv,
+    block_send,
+    block_recv,
+):
+    me = lax.axis_index("dp")
+    rank = lax.axis_index("tensor")
+    high, low = me // 2, lax.rem(me, 2)
+    partner = (me + 1 - 2 * low, rank)
+    nh = n // 2
+    row_peers = [(lax.rem(high + d, nh) * 2 + low, rank) for d in range(1, nh)]
+    x, core = rank // 2, lax.rem(rank, 2)
+    twin = (me, rank + 1 - 2 * core)
+    nx = ranks // 2
+    x_peers = [(me, lax.rem(x + d, nx) * 2 + core) for d in range(1, nx)]
+    greet([partner, twin] + row_peers + x_peers)
+
+    sends = []
+    for d, peer in enumerate([partner] + row_peers):
+        copy = remote(mixed_ref, gathered.at[me], own_send.at[d], take_recv.at[me], peer)
+        copy.start()
+        sends.append(copy)
+    gathered[me] = mixed_ref[...]
+    for d in range(1, nh):
+        source = lax.rem(high - d + nh, nh) * 2 + low
+        spot = gathered.at[source]
+        remote(spot, spot, own_send.at[d], take_recv.at[source], partner).wait_recv()
+        copy = remote(spot, spot, pass_send.at[d], take_recv.at[source], partner)
+        copy.start()
+        sends.append(copy)
+    for d in range(nh):
+        source = lax.rem(high - d + nh, nh) * 2 + 1 - low
+        spot = gathered.at[source]
+        remote(spot, spot, own_send.at[0], take_recv.at[source], partner).wait_recv()
+    for copy in sends:
+        copy.wait_send()
+
+    rows, width = product.shape[3], product.shape[4]
+    chunks = product.shape[0]
+    everything = gathered[...].reshape(n * mixed_ref.shape[0], mixed_ref.shape[1])
+    bufs = (product, half, got, block, landed, (half_send, half_recv, block_send, block_recv))
+    seconds = []
+    for chunk in range(chunks):
+        result = jnp.dot(
+            everything,
+            weight_ref[:, chunk * width : (chunk + 1) * width],
+            preferred_element_type=jnp.float32,
+        )
+        for place in range(ranks):
+            product[chunk, place // 2, place % 2] = result[place * rows : (place + 1) * rows]
+        seconds.append(scatter_sum(chunk, x, core, twin, x_peers, bufs))
+    finishes = [second() for second in seconds]
+    sends = []
+    for chunk in range(chunks):
+        whole[chunk, rank] = finishes[chunk]().astype(jnp.bfloat16)
+        spot = whole.at[chunk, rank]
+        for d, peer in enumerate([twin] + x_peers):
+            copy = remote(spot, spot, end_send.at[chunk, d], end_recv.at[chunk, rank], peer)
+            copy.start()
+            sends.append(copy)
+    for chunk in range(chunks):
+        for d in range(1, nx):
+            source = lax.rem(x - d + nx, nx) * 2 + core
+            spot = whole.at[chunk, source]
+            remote(
+                spot, spot, end_send.at[chunk, d], end_recv.at[chunk, source], twin
+            ).wait_recv()
+            copy = remote(
+                spot, spot, end_pass.at[chunk, d], end_recv.at[chunk, source], twin
+            )
+            copy.start()
+            sends.append(copy)
+    for chunk in range(chunks):
+        for d in range(nx):
+            source = lax.rem(x - d + nx, nx) * 2 + 1 - core
+            spot = whole.at[chunk, source]
+            remote(
+                spot, spot, end_send.at[chunk, 0], end_recv.at[chunk, source], twin
+            ).wait_recv()
+    for copy in sends:
+        copy.wait_send()
+    for chunk in range(chunks):
+        for place in range(ranks):
+            out_ref[place * rows : (place + 1) * rows, chunk * width : (chunk + 1) * width] = whole[
+                chunk, place
+            ]
+
+
+def output(n, ranks, mixed, weight):
+    local, depth = mixed.shape
+    columns = weight.shape[1]
+    width = min(256, columns)
+    chunks = columns // width
+    rows = n * local // ranks
+    vmem = pl.BlockSpec(memory_space=pltpu.VMEM)
+    return pl.pallas_call(
+        functools.partial(output_kernel, n, ranks),
+        out_shape=jax.ShapeDtypeStruct((n * local, columns), jnp.bfloat16),
+        in_specs=[vmem] * 2,
+        out_specs=vmem,
+        scratch_shapes=[
+            pltpu.VMEM((n, local, depth), jnp.bfloat16),
+            pltpu.VMEM((chunks, ranks, rows, width), jnp.bfloat16),
+        ]
+        + sum_scratch(chunks, ranks // 2, rows, width)
+        + [pltpu.SemaphoreType.DMA((n,))] * 3
+        + [pltpu.SemaphoreType.DMA((chunks, ranks))] * 3
+        + sum_sems(chunks, ranks // 2),
+        compiler_params=pltpu.CompilerParams(
+            collective_id=1, has_side_effects=True, vmem_limit_bytes=40 * 1024 * 1024
+        ),
+        cost_estimate=pl.CostEstimate(
+            flops=2 * n * local * depth * columns, bytes_accessed=8000000, transcendentals=0
+        ),
+        name="output",
+    )(mixed, weight)
+
+
 def arrival_ranks(sources):
     ordinal = jnp.arange(sources.shape[-1], dtype=jnp.int32)
     earlier = (sources[..., None, :] == sources[..., :, None]) & (
@@ -164,28 +503,19 @@
         & (my_alive[:, None] > 0)
     ).astype(jnp.bfloat16)
 
-    hidden_float = hidden_in.astype(jnp.float32)
-    inverse = lax.rsqrt(jnp.mean(hidden_float * hidden_float, axis=1) + 1e-06)
-    blocked = lax.all_to_all(hidden_in, "dp", split_axis=1, concat_axis=0, tiled=True)
-    scaled = (blocked.astype(jnp.float32) * norm_gain.astype(jnp.float32)[None, :]).astype(
-        jnp.bfloat16
-    )
-    partial = jnp.concatenate(
-        [
-            jnp.dot(scaled, weight, preferred_element_type=jnp.float32).astype(jnp.bfloat16)
-            for weight in (query_weight, key_weight, value_weight)
-        ],
-        axis=1,
-    ).reshape(device_count, local_beams, query_width + 2 * key_width)
-    partial = lax.all_to_all(partial, "dp", split_axis=0, concat_axis=0, tiled=True)
-    summed = jnp.sum(partial.astype(jnp.float32), axis=0) * inverse[:, None]
-    heads = summed.reshape(local_beams, row_count, HEAD_DIM)
-    turned = rotate(heads[:, : head_count + group_count], position)
-    fresh = jnp.concatenate([turned, heads[:, head_count + group_count :]], axis=1).astype(
-        jnp.bfloat16
+    cosine, sine = turn_angles(position)
+    fresh = project(
+        device_count,
+        hidden_in,
+        norm_gain[None, :],
+        query_weight,
+        key_weight,
+        value_weight,
+        cosine,
+        sine,
     )
     packed = jnp.dot(
-        placing, fresh.reshape(local_beams, row_count * HEAD_DIM), preferred_element_type=jnp.float32
+        placing, fresh, preferred_element_type=jnp.float32
     ).astype(jnp.bfloat16)
     arrived = lax.all_to_all(
         packed.reshape(device_count, capacity, row_count, HEAD_DIM),
@@ -201,15 +531,7 @@
     attention = jnp.dot(
         picking, back.reshape(slot_total, query_width), preferred_element_type=jnp.float32
     ).astype(jnp.bfloat16)
-    gathered = lax.all_to_all(
-        jnp.broadcast_to(attention[None], (device_count,) + attention.shape),
-        "dp",
-        split_axis=0,
-        concat_axis=0,
-        tiled=True,
-    ).reshape(device_count * local_beams, query_width)
-    partial_sum = jnp.dot(gathered, output_weight, preferred_element_type=jnp.float32)
-    return lax.psum(partial_sum, "tensor").astype(jnp.bfloat16)
+    return output(device_count, lax.axis_size("tensor"), attention, output_weight)
 
 
 def solution(mesh):

time: 164 us -> 118 us (0.72)
  Pallas kernels: 7.96 us -> 73.8 us
  blocking collectives: 54.3 us -> 0 us
  waiting for transfers between devices: 53.5 us -> 8.73 us
  starting transfers between devices: 19.7 us -> 8.89 us
  matrix products: 8.72 us -> 1.17 us
  local copies, waits for them, and re-layouts: 14.9 us -> 22.4 us
  other arithmetic: 3.98 us -> 1.94 us
    pallas_call x0 -> x2, Pallas kernels: none -> 65.8 us  [the longest x1 35.8 us: project(): pl.pallas_call(functools.partial(project_kernel, n), out_shape=jax.ShapeD...]
    all_to_all x2 -> x0, waiting for transfers between devices: 44.3 us -> none  [the longest x1 30.5 us: body(): lax.all_to_all(partial, 'dp', split_axis=0, concat_axis=0, tiled=True)]
    all_to_all x1 -> x0, blocking collectives: 28.7 us -> none  [body(): lax.all_to_all(jnp.broadcast_to(attention[None], (device_count,) + attent...]
    psum x1 -> x0, blocking collectives: 25.6 us -> none  [body(): return lax.psum(partial_sum, 'tensor').astype(jnp.bfloat16)]
    all_to_all x2 -> x0, starting transfers between devices: 10.9 us -> none  [the longest x1 7.28 us: body(): lax.all_to_all(hidden_in, 'dp', split_axis=1, concat_axis=0, tiled=True)]
    unnamed x15 -> x16, local copies, waits for them, and re-layouts: 12.4 us -> 20.7 us
    dot_general x5 -> x1, matrix products: 8.5 us -> 0.95 us  [body(): jnp.dot(placing, fresh, preferred_element_type=jnp.float32)]
    all_to_all x1 -> x0, local copies, waits for them, and re-layouts: 1.96 us -> none  [body(): lax.all_to_all(hidden_in, 'dp', split_axis=1, concat_axis=0, tiled=True)]
  transfers between devices with their start and end apart: 4 -> 2, of which waited for: 4 -> 2; matrix products, arithmetic and copies ran while one was open for 7% -> 8% of each run, Pallas kernels for 0% -> 0%
where the time goes in v2:
time: 118 us; the launch traced here: 117 us
  Pallas kernels  73.8 us (63%)
  local copies, waits for them, and re-layouts  22.4 us (19%)
  starting transfers between devices  8.89 us (8%)
  waiting for transfers between devices  8.73 us (7%)
  other arithmetic  1.94 us (2%)
    pallas_call x1, Pallas kernels, project(): pl.pallas_call(functools.partial(project_kernel, n), out_shape=jax.ShapeD...  35.8 us
    pallas_call x1, Pallas kernels, output(): pl.pallas_call(functools.partial(output_kernel, n, ranks), out_shape=jax....  29.9 us
    unnamed x16, local copies, waits for them, and re-layouts  20.7 us
    all_to_all x1, waiting for transfers between devices, body(): back = lax.all_to_all(mixed, 'dp', split_axis=0, concat_axis=0, tiled=True)  8.25 us
    pallas_call x1, Pallas kernels, attend(): pl.pallas_call(functools.partial(attend_kernel, capacity, head_count), gr...  7.96 us
    all_to_all x1, starting transfers between devices, body(): back = lax.all_to_all(mixed, 'dp', split_axis=0, concat_axis=0, tiled=True)  5.46 us
    all_to_all x1, starting transfers between devices, body(): lax.all_to_all(packed.reshape(device_count, capacity, row_count, HEAD_DIM...  3.43 us
  transfers between devices with their start and end apart: 2, of which 2 were waited for; matrix products, arithmetic and copies ran while one was open for 8% of the time, Pallas kernels for 0%

profile of v2, /device:TPU:0, one launch (start us, length us, event | category | flops | bytes accessed | tf_op | source)
XLA Modules:
  0.0 117.0 jit_solution(11178046441723896646)
XLA Ops:
  0.0 0.8 reshape.141
  0.8 0.9 select_reduce_fusion
  1.7 0.7 broadcast_in_dim.60.gain_ref
  2.4 0.1 dynamic-slice_convert_fusion
  2.4 0.3 convert_reduce_fusion
  2.8 0.1 fusion.9
  2.9 0.1 pad_maximum_fusion
  3.0 2.2 %copy-done.1 = bf16[1024,2048]{1,0:T(8,128)(2,1)S(1)} copy-done((bf16[1024,2048]{1,0:T(8,128)(2,1)S(1)}, bf16[1024,2048]{1,0:T(8,128)(2,1)}, u32[]{:S(2)}) %copy-start.1) | copy-done | bytes 4194328
  5.2 1.0 copy-done.3
  6.2 1.0 copy-done.4
  7.3 1.0 copy-done.5
  8.3 35.8 %project.1 = bf16[32,2560]{1,0:T(8,128)(2,1)S(1)} custom-call(bf16[32,8192]{1,0:T(8,128)(2,1)S(1)} %copy-done.3, bf16[1,1024]{1,0:T(2,128)(2,1)S(1)} %broadcast_in_dim.60.gain_ref, bf16[1024,2048]{1,0:T(8,128)(2,1)S(1)} %copy-done.1, bf16[1024,256]{1,0:T(8,128)(2,1)S(1)} %copy-done.4, bf16[1024,256]{1,0:T(8,128)(2,1)S(1)} %copy-done.5, ...), custom_call_target="tpu_custom_call" | custom-call | flops 1342177280 | bytes 8000000 | tf_op jit(solution)/shard_map/project/pallas_call | solution.py:288
  44.1 0.9 fusion
  45.1 3.4 %all-to-all-start = ((bf16[8,8,20,128]{3,1,2,0:T(8,128)(2,1)}), bf16[8,8,20,128]{3,1,2,0:T(8,128)(2,1)S(1)}, u32[]{:S(2)}, u32[]{:S(2)}) async-start(bf16[8,8,20,128]{3,1,2,0:T(8,128)(2,1)} %fusion), calls=%async_computation | async-start | bytes 655360 | tf_op jit(solution)/shard_map/all_to_all | solution.py:520
  48.5 0.1 broadcast_in_dim.58
  48.6 0.3 select_reduce_fusion.1
  49.0 0.1 reshape.143.length_ref
  49.1 0.1 reshape.142.parent_ref
  49.1 9.0 %copy.24 = bf16[32,256,2,2,128]{4,1,3,2,0:T(8,128)(2,1)} copy(bf16[32,256,2,2,128]{4,3,2,1,0:T(2,128)(2,1)} %param.16) | data formatting | bytes 16777216 | tf_op args[6]
  58.1 0.5 all-to-all-done
  58.6 0.1 copy.17.new_ref
  58.7 0.0 copy-start
  58.7 3.4 %copy-done = bf16[32,256,2,2,128]{4,1,3,2,0:T(8,128)(2,1)S(1)} copy-done((bf16[32,256,2,2,128]{4,1,3,2,0:T(8,128)(2,1)S(1)}, bf16[32,256,2,2,128]{4,1,3,2,0:T(8,128)(2,1)}, u32[]{:S(2)}) %copy-start) | copy-done | bytes 8388632
  62.1 8.0 %attend.1 = bf16[8,8,16,128]{3,2,1,0:T(8,128)(2,1)} custom-call(s32[64]{0:T(128)S(1)} %reshape.142.parent_ref, s32[64]{0:T(128)S(1)} %reshape.143.length_ref, bf16[8,8,20,128]{3,2,1,0:T(8,128)(2,1)S(1)} %copy.17.new_ref, bf16[32,2,2,256,128]{4,3,2,1,0:T(8,128)(2,1)S(1)} %bitcast.13), custom_call_target="tpu_custom_call" | custom-call | tf_op jit(solution)/shard_map/attend/pallas_call | solution.py:91
  70.0 5.5 %all-to-all-start.1 = ((bf16[8,8,16,128]{3,2,1,0:T(8,128)(2,1)}), bf16[8,8,16,128]{3,2,1,0:T(8,128)(2,1)S(1)}, u32[]{:S(2)}, u32[]{:S(2)}) async-start(bf16[8,8,16,128]{3,2,1,0:T(8,128)(2,1)} %attend.1), calls=%async_computation.1 | async-start | bytes 524288 | tf_op jit(solution)/shard_map/all_to_all | solution.py:530
  75.5 0.1 dynamic-slice_compare_fusion
  75.6 8.3 %all-to-all-done.1 = bf16[8,8,16,128]{3,2,1,0:T(8,128)(2,1)S(1)} async-done(((bf16[8,8,16,128]{3,2,1,0:T(8,128)(2,1)}), bf16[8,8,16,128]{3,2,1,0:T(8,128)(2,1)S(1)}, u32[]{:S(2)}, u32[]{:S(2)}) %all-to-all-start.1) | async-done | bytes 262176 | tf_op jit(solution)/shard_map/all_to_all | solution.py:530
  83.8 0.2 convolution_convert_fusion.1.mixed_ref
  84.1 0.0 copy-start.2
  84.1 2.2 %copy-done.2 = bf16[2048,1024]{1,0:T(8,128)(2,1)S(1)} copy-done((bf16[2048,1024]{1,0:T(8,128)(2,1)S(1)}, bf16[2048,1024]{1,0:T(8,128)(2,1)}, u32[]{:S(2)}) %copy-start.2) | copy-done | bytes 4194328
  86.3 29.9 %output.1 = bf16[256,1024]{1,0:T(8,128)(2,1)S(1)} custom-call(bf16[32,2048]{1,0:T(8,128)(2,1)S(1)} %convolution_convert_fusion.1.mixed_ref, bf16[2048,1024]{1,0:T(8,128)(2,1)S(1)} %copy-done.2), custom_call_target="tpu_custom_call" | custom-call | flops 1073741824 | bytes 8000000 | tf_op jit(solution)/shard_map/output/pallas_call | solution.py:421
  116.2 0.8 copy.26
  (11 shorter events, 0.1 us)
Async XLA Ops:
  3.0 2.2 %copy-start.1 = (bf16[1024,2048]{1,0:T(8,128)(2,1)S(1)}, bf16[1024,2048]{1,0:T(8,128)(2,1)}, u32[]{:S(2)}) copy-start(bf16[1024,2048]{1,0:T(8,128)(2,1)} %query_ref.1) | copy-start | bytes 12582916
  5.2 1.0 copy-start.3
  6.2 1.0 copy-start.4
  7.3 1.0 copy-start.5
  45.1 13.5 %all-to-all-start = ((bf16[8,8,20,128]{3,1,2,0:T(8,128)(2,1)}), bf16[8,8,20,128]{3,1,2,0:T(8,128)(2,1)S(1)}, u32[]{:S(2)}, u32[]{:S(2)}) async-start(bf16[8,8,20,128]{3,1,2,0:T(8,128)(2,1)} %fusion), calls=%async_computation | async-start | bytes 655360 | tf_op jit(solution)/shard_map/all_to_all | solution.py:520
  58.1 17.4 %copy-start.6 = (s32[256]{0:T(256)S(1)}, s32[256]{0:T(256)}, u32[]{:S(2)}) copy-start(s32[256]{0:T(256)} %param.19) | copy-start | bytes 3076
  58.7 3.4 %copy-start = (bf16[32,256,2,2,128]{4,1,3,2,0:T(8,128)(2,1)S(1)}, bf16[32,256,2,2,128]{4,1,3,2,0:T(8,128)(2,1)}, u32[]{:S(2)}) copy-start(bf16[32,256,2,2,128]{4,1,3,2,0:T(8,128)(2,1)} %copy.24) | copy-start | bytes 25165828
  70.0 13.8 %all-to-all-start.1 = ((bf16[8,8,16,128]{3,2,1,0:T(8,128)(2,1)}), bf16[8,8,16,128]{3,2,1,0:T(8,128)(2,1)S(1)}, u32[]{:S(2)}, u32[]{:S(2)}) async-start(bf16[8,8,16,128]{3,2,1,0:T(8,128)(2,1)} %attend.1), calls=%async_computation.1 | async-start | bytes 524288 | tf_op jit(solution)/shard_map/all_to_all | solution.py:530
  84.1 2.2 %copy-start.2 = (bf16[2048,1024]{1,0:T(8,128)(2,1)S(1)}, bf16[2048,1024]{1,0:T(8,128)(2,1)}, u32[]{:S(2)}) copy-start(bf16[2048,1024]{1,0:T(8,128)(2,1)} %weight_ref.1) | copy-start | bytes 12582916

commit v3 on v2

--- a/solution.py
+++ b/solution.py
@@ -78,13 +78,12 @@
 
 def attend(parents, lengths, arrived, cache, head_count):
     device_count, capacity, rows, _ = arrived.shape
-    whole = cache.shape
     spec = pltpu.PrefetchScalarGridSpec(
         num_scalar_prefetch=2,
         grid=(device_count,),
         in_specs=[
             pl.BlockSpec((1, capacity, rows, HEAD_DIM), lambda i, *_: (i, 0, 0, 0)),
-            pl.BlockSpec(whole, lambda i, *_: (0, 0, 0, 0, 0)),
+            pl.BlockSpec(memory_space=pltpu.VMEM),
         ],
         out_specs=pl.BlockSpec((1, capacity, head_count, HEAD_DIM), lambda i, *_: (i, 0, 0, 0)),
     )
@@ -169,7 +168,19 @@
     value_ref,
     cosine_ref,
     sine_ref,
+    placing_ref,
+    cache_ref,
     out_ref,
+    sorted_ref,
+    hidden_own,
+    query_own,
+    tail_own,
+    raw,
+    packed,
+    arrive,
+    load_sems,
+    slot_send,
+    slot_recv,
     blocks,
     product,
     half,
@@ -188,6 +199,7 @@
     me = lax.axis_index("dp")
     rank = lax.axis_index("tensor")
     core = lax.rem(rank, 2)
+    capacity = placing_ref.shape[0] // n
     twin = (me, rank + 1 - 2 * core)
     high, low = me // 2, lax.rem(me, 2)
     partner = (me + 1 - 2 * low, rank)
@@ -195,6 +207,21 @@
     others = [(lax.rem(me + d, n), rank) for d in range(1, n)]
     rows, depth = hidden_ref.shape[0], query_ref.shape[0]
     part = rows // 2
+    key_width = key_ref.shape[1]
+    loads = [
+        pltpu.make_async_copy(source, target, load_sems.at[at])
+        for at, (source, target) in enumerate(
+            [
+                (hidden_ref, hidden_own),
+                (cache_ref, raw),
+                (query_ref, query_own),
+                (key_ref, tail_own.at[:, :key_width]),
+                (value_ref, tail_own.at[:, key_width:]),
+            ]
+        )
+    ]
+    for load in loads:
+        load.start()
     greet(others + [twin])
     mine = pl.ds(pl.multiple_of(core * part, part), part)
     theirs = pl.ds(pl.multiple_of((1 - core) * part, part), part)
@@ -211,11 +238,38 @@
         )
         copy.start()
         moves.append(copy)
-    blocks[0] = hidden_ref[:, pl.ds(pl.multiple_of(me * depth, depth), depth)]
-    hidden = hidden_ref[...].astype(jnp.float32)
+    loads[0].wait()
+    blocks[0] = hidden_own[:, pl.ds(pl.multiple_of(me * depth, depth), depth)]
+    hidden = hidden_own[...].astype(jnp.float32)
     inverse = lax.rsqrt(
         jnp.sum(hidden * hidden, axis=1, keepdims=True) / hidden_ref.shape[1] + 1e-06
     )
+    loads[1].wait()
+    kinds = 2 * sorted_ref.shape[2]
+    span = 256
+    each = span // kinds
+    to = lax.broadcasted_iota(jnp.int32, (span, span), 0)
+    of = lax.broadcasted_iota(jnp.int32, (span, span), 1)
+    order = (of == kinds * (to % each) + to // each).astype(jnp.bfloat16)
+
+    def sort_beam(beam, carry):
+        for piece in range(raw.shape[1] // span):
+            moved = jnp.dot(
+                order,
+                raw[beam, piece * span : (piece + 1) * span, :],
+                preferred_element_type=jnp.float32,
+            ).astype(jnp.bfloat16)
+            for kind in range(kinds):
+                sorted_ref[
+                    beam,
+                    kind // sorted_ref.shape[2],
+                    kind % sorted_ref.shape[2],
+                    piece * each : (piece + 1) * each,
+                    :,
+                ] = moved[kind * each : (kind + 1) * each]
+        return carry
+
+    lax.fori_loop(0, raw.shape[0], sort_beam, 0)
     passes = []
     for d in range(1, n):
         moves[d - 1].wait_recv()
@@ -238,11 +292,13 @@
     chunks = product.shape[0]
     bufs = (product, half, got, block, landed, (half_send, half_recv, block_send, block_recv))
     seconds = []
+    for load in loads[2:]:
+        load.wait()
     for chunk in range(chunks):
         if chunk < chunks - 1:
-            weight = query_ref[:, chunk * width : (chunk + 1) * width]
+            weight = query_own[:, chunk * width : (chunk + 1) * width]
         else:
-            weight = jnp.concatenate([key_ref[...], value_ref[...]], axis=1)
+            weight = tail_own[...]
         result = jnp.dot(scaled, weight, preferred_element_type=jnp.float32)
         for d in range(n):
             owner = lax.rem(me - d + n, n)
@@ -257,7 +313,30 @@
             if chunk < chunks - 1 or first < width // 2:
                 vector = vector * cosine + pltpu.roll(vector, HEAD_DIM // 2, 1) * sine
             at = chunk * width + first
-            out_ref[:, at : at + HEAD_DIM] = vector.astype(jnp.bfloat16)
+            vector = jnp.dot(
+                placing_ref[...], vector.astype(jnp.bfloat16), preferred_element_type=jnp.float32
+            )
+            for d in range(n):
+                packed[d, :, at : at + HEAD_DIM] = vector[
+                    d * capacity : (d + 1) * capacity
+                ].astype(jnp.bfloat16)
+    copies = []
+    for d in range(1, n):
+        target = lax.rem(me + d, n)
+        copy = remote(
+            packed.at[target], arrive.at[me], slot_send.at[d], slot_recv.at[d], (target, rank)
+        )
+        copy.start()
+        copies.append(copy)
+    arrive[me] = packed[me]
+    for copy in copies:
+        copy.wait_send()
+    for d in range(1, n):
+        source = lax.rem(me - d + n, n)
+        remote(
+            packed.at[source], arrive.at[source], slot_send.at[d], slot_recv.at[d], (source, rank)
+        ).wait_recv()
+    out_ref[...] = arrive[...]
 
 
 def sum_scratch(chunks, nh, rows, width):
@@ -279,37 +358,64 @@
     ]
 
 
-def project(n, hidden, gain, query_weight, key_weight, value_weight, cosine, sine):
+def project(
+    n, hidden, gain, query_weight, key_weight, value_weight, cosine, sine, placing, cache
+):
     rows = hidden.shape[0]
     depth, query_width = query_weight.shape
     width = 2 * key_weight.shape[1]
     chunks = query_width // width + 1
+    capacity = placing.shape[0] // n
+    beams, length, _, groups, _ = cache.shape
+    flat = cache.reshape(beams, length * 2 * groups, HEAD_DIM)
     vmem = pl.BlockSpec(memory_space=pltpu.VMEM)
+    hbm = pl.BlockSpec(memory_space=pl.ANY)
     return pl.pallas_call(
         functools.partial(project_kernel, n),
-        out_shape=jax.ShapeDtypeStruct((rows, chunks * width), jnp.bfloat16),
-        in_specs=[vmem] * 7,
-        out_specs=vmem,
-        scratch_shapes=[pltpu.VMEM((n, rows, depth), jnp.bfloat16)]
+        out_shape=[
+            jax.ShapeDtypeStruct((n, capacity, chunks * width), jnp.bfloat16),
+            jax.ShapeDtypeStruct((beams, 2, groups, length, HEAD_DIM), jnp.bfloat16),
+        ],
+        in_specs=[hbm, vmem, hbm, hbm, hbm, vmem, vmem, vmem, hbm],
+        out_specs=[vmem, vmem],
+        scratch_shapes=[
+            pltpu.VMEM(hidden.shape, jnp.bfloat16),
+            pltpu.VMEM(query_weight.shape, jnp.bfloat16),
+            pltpu.VMEM((depth, width), jnp.bfloat16),
+            pltpu.VMEM(flat.shape, jnp.bfloat16),
+            pltpu.VMEM((n, capacity, chunks * width), jnp.bfloat16),
+            pltpu.VMEM((n, capacity, chunks * width), jnp.bfloat16),
+            pltpu.SemaphoreType.DMA((5,)),
+            pltpu.SemaphoreType.DMA((n,)),
+            pltpu.SemaphoreType.DMA((n,)),
+            pltpu.VMEM((n, rows, depth), jnp.bfloat16),
+        ]
         + sum_scratch(chunks, n // 2, rows, width)
         + [pltpu.SemaphoreType.DMA((n,))] * 4
         + sum_sems(chunks, n // 2),
         compiler_params=pltpu.CompilerParams(
-            collective_id=0, has_side_effects=True, vmem_limit_bytes=40 * 1024 * 1024
+            collective_id=0, has_side_effects=True, vmem_limit_bytes=56 * 1024 * 1024
         ),
         cost_estimate=pl.CostEstimate(
             flops=2 * n * rows * depth * chunks * width, bytes_accessed=8000000, transcendentals=0
         ),
         name="project",
-    )(hidden, gain, query_weight, key_weight, value_weight, cosine, sine)
+    )(hidden, gain, query_weight, key_weight, value_weight, cosine, sine, placing, flat)
 
 
 def output_kernel(
     n,
     ranks,
-    mixed_ref,
+    slots_ref,
+    picking_ref,
     weight_ref,
     out_ref,
+    weight_own,
+    back,
+    mixed_ref,
+    load_sem,
+    slot_send,
+    slot_recv,
     gathered,
     whole,
     product,
@@ -338,7 +444,29 @@
     twin = (me, rank + 1 - 2 * core)
     nx = ranks // 2
     x_peers = [(me, lax.rem(x + d, nx) * 2 + core) for d in range(1, nx)]
-    greet([partner, twin] + row_peers + x_peers)
+    load = pltpu.make_async_copy(weight_ref, weight_own, load_sem.at[0])
+    load.start()
+    greet([twin] + x_peers + [(lax.rem(me + d, n), rank) for d in range(1, n)])
+    copies = []
+    for d in range(1, n):
+        target = lax.rem(me + d, n)
+        copy = remote(
+            slots_ref.at[target], back.at[me], slot_send.at[d], slot_recv.at[d], (target, rank)
+        )
+        copy.start()
+        copies.append(copy)
+    back[me] = slots_ref[me]
+    for d in range(1, n):
+        source = lax.rem(me - d + n, n)
+        remote(
+            slots_ref.at[source], back.at[source], slot_send.at[d], slot_recv.at[d], (source, rank)
+        ).wait_recv()
+    held = jnp.concatenate([back[d].astype(jnp.float32) for d in range(n)], axis=0)
+    mixed_ref[...] = jnp.dot(
+        picking_ref[...], held.astype(jnp.bfloat16), preferred_element_type=jnp.float32
+    ).astype(jnp.bfloat16)
+    for copy in copies:
+        copy.wait_send()
 
     sends = []
     for d, peer in enumerate([partner] + row_peers):
@@ -362,13 +490,14 @@
 
     rows, width = product.shape[3], product.shape[4]
     chunks = product.shape[0]
+    load.wait()
     everything = gathered[...].reshape(n * mixed_ref.shape[0], mixed_ref.shape[1])
     bufs = (product, half, got, block, landed, (half_send, half_recv, block_send, block_recv))
     seconds = []
     for chunk in range(chunks):
         result = jnp.dot(
             everything,
-            weight_ref[:, chunk * width : (chunk + 1) * width],
+            weight_own[:, chunk * width : (chunk + 1) * width],
             preferred_element_type=jnp.float32,
         )
         for place in range(ranks):
@@ -411,8 +540,9 @@
             ]
 
 
-def output(n, ranks, mixed, weight):
-    local, depth = mixed.shape
+def output(n, ranks, slots, picking, weight):
+    depth = slots.shape[2]
+    local = picking.shape[0]
     columns = weight.shape[1]
     width = min(256, columns)
     chunks = columns // width
@@ -421,9 +551,15 @@
     return pl.pallas_call(
         functools.partial(output_kernel, n, ranks),
         out_shape=jax.ShapeDtypeStruct((n * local, columns), jnp.bfloat16),
-        in_specs=[vmem] * 2,
+        in_specs=[vmem, vmem, pl.BlockSpec(memory_space=pl.ANY)],
         out_specs=vmem,
         scratch_shapes=[
+            pltpu.VMEM(weight.shape, jnp.bfloat16),
+            pltpu.VMEM(slots.shape, jnp.bfloat16),
+            pltpu.VMEM((local, depth), jnp.bfloat16),
+            pltpu.SemaphoreType.DMA((1,)),
+            pltpu.SemaphoreType.DMA((n,)),
+            pltpu.SemaphoreType.DMA((n,)),
             pltpu.VMEM((n, local, depth), jnp.bfloat16),
             pltpu.VMEM((chunks, ranks, rows, width), jnp.bfloat16),
         ]
@@ -432,13 +568,13 @@
         + [pltpu.SemaphoreType.DMA((chunks, ranks))] * 3
         + sum_sems(chunks, ranks // 2),
         compiler_params=pltpu.CompilerParams(
-            collective_id=1, has_side_effects=True, vmem_limit_bytes=40 * 1024 * 1024
+            collective_id=1, has_side_effects=True, vmem_limit_bytes=56 * 1024 * 1024
         ),
         cost_estimate=pl.CostEstimate(
             flops=2 * n * local * depth * columns, bytes_accessed=8000000, transcendentals=0
         ),
         name="output",
-    )(mixed, weight)
+    )(slots, picking, weight)
 
 
 def arrival_ranks(sources):
@@ -472,8 +608,6 @@
     group_count = key_width // HEAD_DIM
     row_count = head_count + 2 * group_count
 
-    cache = jnp.transpose(key_value_cache, (0, 2, 3, 1, 4))
-
     all_parents = parent_beam.reshape(device_count, local_beams)
     all_sources = all_parents // local_beams
     all_ranks = arrival_ranks(all_sources)
@@ -504,7 +638,7 @@
     ).astype(jnp.bfloat16)
 
     cosine, sine = turn_angles(position)
-    fresh = project(
+    arrived, cache = project(
         device_count,
         hidden_in,
         norm_gain[None, :],
@@ -513,25 +647,15 @@
         value_weight,
         cosine,
         sine,
-    )
-    packed = jnp.dot(
-        placing, fresh, preferred_element_type=jnp.float32
-    ).astype(jnp.bfloat16)
-    arrived = lax.all_to_all(
-        packed.reshape(device_count, capacity, row_count, HEAD_DIM),
-        "dp",
-        split_axis=0,
-        concat_axis=0,
-        tiled=True,
-    )
+        placing,
+        key_value_cache,
+    )
+    arrived = arrived.reshape(device_count, capacity, row_count, HEAD_DIM)
     mixed = attend(
         slot_parent.reshape(-1), slot_length.reshape(-1), arrived, cache, head_count
     )
-    back = lax.all_to_all(mixed, "dp", split_axis=0, concat_axis=0, tiled=True)
-    attention = jnp.dot(
-        picking, back.reshape(slot_total, query_width), preferred_element_type=jnp.float32
-    ).astype(jnp.bfloat16)
-    return output(device_count, lax.axis_size("tensor"), attention, output_weight)
+    slots = mixed.reshape(device_count, capacity, query_width)
+    return output(device_count, lax.axis_size("tensor"), slots, picking, output_weight)
 
 
 def solution(mesh):

time: 118 us -> 114 us (0.966)
  Pallas kernels: 73.8 us -> 98.5 us
  local copies, waits for them, and re-layouts: 22.4 us -> 9.41 us
  starting transfers between devices: 8.89 us -> 0 us
  waiting for transfers between devices: 8.73 us -> 0 us
  other arithmetic: 1.94 us -> 3.83 us
    unnamed x16 -> x5, local copies, waits for them, and re-layouts: 20.7 us -> 5.25 us
    pallas_call x1, Pallas kernels: 35.8 us -> 50.1 us  [project(): pl.pallas_call(functools.partial(project_kernel, n), out_shape=[jax.Shape...]
    pallas_call x1, Pallas kernels: 29.9 us -> 41.2 us  [output(): pl.pallas_call(functools.partial(output_kernel, n, ranks), out_shape=jax....]
    all_to_all x2 -> x0, starting transfers between devices: 8.89 us -> none  [the longest x1 5.46 us: body(): back = lax.all_to_all(mixed, 'dp', split_axis=0, concat_axis=0, tiled=True)]
    all_to_all x2 -> x0, waiting for transfers between devices: 8.73 us -> none  [the longest x1 8.25 us: body(): back = lax.all_to_all(mixed, 'dp', split_axis=0, concat_axis=0, tiled=True)]
    reshape x0 -> x2, local copies, waits for them, and re-layouts: none -> 1.87 us  [the longest x1 1.05 us: body(): arrived = arrived.reshape(device_count, capacity, row_count, HEAD_DIM)]
    convert_element_type x0 -> x2, other arithmetic: none -> 1.28 us  [the longest x1 0.67 us: body(): picking = ((jnp.arange(slot_total, dtype=jnp.int32)[None, :] == target[:,...]
  transfers between devices with their start and end apart: 2 -> 0, of which waited for: 2 -> 0; matrix products, arithmetic and copies ran while one was open for 8% -> 0% of each run, Pallas kernels for 0% -> 0%
where the time goes in v3:
time: 114 us; the launch traced here: 112 us
  Pallas kernels  98.5 us (86%)
  local copies, waits for them, and re-layouts  9.41 us (8%)
  other arithmetic  3.83 us (3%)
    pallas_call x1, Pallas kernels, project(): pl.pallas_call(functools.partial(project_kernel, n), out_shape=[jax.Shape...  50.1 us
    pallas_call x1, Pallas kernels, output(): pl.pallas_call(functools.partial(output_kernel, n, ranks), out_shape=jax....  41.2 us
    pallas_call x1, Pallas kernels, attend(): pl.pallas_call(functools.partial(attend_kernel, capacity, head_count), gr...  7.32 us
    unnamed x5, local copies, waits for them, and re-layouts  5.25 us

profile of v3, /device:TPU:0, one launch (start us, length us, event | category | flops | bytes accessed | tf_op | source)
XLA Modules:
  0.0 111.9 jit_solution(13279711144846949487)
XLA Ops:
  0.0 0.9 select_reduce_fusion
  0.9 0.1 broadcast_in_dim.58
  1.0 0.8 reshape.144
  1.7 0.3 convert_reduce_fusion
  2.1 0.3 select_reduce_fusion.1
  2.4 0.1 reshape.145.parent_ref
  2.5 0.1 reshape.146.length_ref
  2.6 1.3 %broadcast_in_dim.60.gain_ref = bf16[1,1024]{1,0:T(2,128)(2,1)} reshape(bf16[1024]{0:T(1024)(128)(2,1)} %param.11) | data formatting | bytes 4096 | tf_op jit(solution)/shard_map/broadcast_in_dim | solution.py:644
  3.9 0.1 dynamic-slice_convert_fusion
  3.9 0.1 fusion.4
  4.1 0.7 pad_maximum_fusion
  4.8 0.6 fusion.1.placing_ref
  5.4 50.1 %project.1 = (bf16[8,8,2560]{2,1,0:T(8,128)(2,1)}, bf16[32,2,2,256,128]{4,3,2,1,0:T(8,128)(2,1)}) custom-call(bf16[32,8192]{1,0:T(8,128)(2,1)} %hidden_ref.1, bf16[1,1024]{1,0:T(2,128)(2,1)} %broadcast_in_dim.60.gain_ref, bf16[1024,2048]{1,0:T(8,128)(2,1)} %query_ref.1, bf16[1024,256]{1,0:T(8,128)(2,1)} %key_ref.1, bf16[1024,256]{1,0:T(8,128)(2,1)} %value_ref.1, ...), custom_call_target="tpu_custom_call" | custom-call | flops 1342177280 | bytes 8000000 | tf_op jit(solution)/shard_map/project/pallas_call | solution.py:373
  55.5 0.0 copy-start.1
  55.5 1.0 copy.12.new_ref
  56.5 0.0 copy-start
  56.6 3.4 %copy-done = bf16[32,2,2,256,128]{4,3,2,1,0:T(8,128)(2,1)S(1)} copy-done((bf16[32,2,2,256,128]{4,3,2,1,0:T(8,128)(2,1)S(1)}, bf16[32,2,2,256,128]{4,3,2,1,0:T(8,128)(2,1)}, u32[]{:S(2)}) %copy-start) | copy-done | bytes 8388632
  59.9 7.3 %attend.1 = bf16[8,8,16,128]{3,2,1,0:T(8,128)(2,1)S(1)} custom-call(s32[64]{0:T(128)S(1)} %reshape.145.parent_ref, s32[64]{0:T(128)S(1)} %reshape.146.length_ref, bf16[8,8,20,128]{3,2,1,0:T(8,128)(2,1)S(1)} %copy.12.new_ref, bf16[32,2,2,256,128]{4,3,2,1,0:T(8,128)(2,1)S(1)} %copy-done), custom_call_target="tpu_custom_call" | custom-call | tf_op jit(solution)/shard_map/attend/pallas_call | solution.py:90
  67.2 0.8 reshape.149.slots_ref
  68.1 0.0 copy-done.1
  68.1 0.1 dynamic-slice_compare_fusion
  68.2 0.7 fusion.3.picking_ref
  68.8 41.2 %output.1 = bf16[256,1024]{1,0:T(8,128)(2,1)} custom-call(bf16[8,8,2048]{2,1,0:T(8,128)(2,1)} %reshape.149.slots_ref, bf16[32,64]{1,0:T(8,128)(2,1)} %fusion.3.picking_ref, bf16[2048,1024]{1,0:T(8,128)(2,1)} %weight_ref.1), custom_call_target="tpu_custom_call" | custom-call | flops 1073741824 | bytes 8000000 | tf_op jit(solution)/shard_map/output/pallas_call | solution.py:551
  110.0 1.9 %copy.14 = bf16[256,1024]{1,0:T(8,128)(2,1)} copy(bf16[256,1024]{1,0:T(8,128)(2,1)} %output.1) | data formatting | bytes 1048576
  (5 shorter events, 0.0 us)
Async XLA Ops:
  55.5 12.6 %copy-start.1 = (s32[256]{0:T(256)S(1)}, s32[256]{0:T(256)}, u32[]{:S(2)}) copy-start(s32[256]{0:T(256)} %param.19) | copy-start | bytes 3076
  56.5 3.4 %copy-start = (bf16[32,2,2,256,128]{4,3,2,1,0:T(8,128)(2,1)S(1)}, bf16[32,2,2,256,128]{4,3,2,1,0:T(8,128)(2,1)}, u32[]{:S(2)}) copy-start(bf16[32,2,2,256,128]{4,3,2,1,0:T(8,128)(2,1)} %get-tuple-element.8.cache_ref) | copy-start | bytes 25165828

commit v4 on v3

--- a/solution.py
+++ b/solution.py
@@ -23,21 +23,20 @@
     )
 
 
-def attend_kernel(capacity, head_count, parent_ref, length_ref, new_ref, cache_ref, out_ref):
-    groups = cache_ref.shape[2]
-    length = cache_ref.shape[3]
+def attend_kernel(capacity, head_count, parent_ref, length_ref, new_ref, *refs):
+    caches, out_ref = refs[:capacity], refs[capacity]
+    groups = caches[0].shape[2]
     per_group = head_count // groups
     first = pl.program_id(0) * capacity
     score_scale = 1.0 / math.sqrt(HEAD_DIM)
     rows = groups * per_group
     scores, latest, limits = [], [], []
     for slot in range(capacity):
-        parent = parent_ref[first + slot]
         limits.append(jnp.full((rows, 1), length_ref[first + slot], jnp.int32))
         for group in range(groups):
             query = new_ref[0, slot, group * per_group : (group + 1) * per_group, :]
             key_row = new_ref[0, slot, head_count + group : head_count + group + 1, :]
-            keys = cache_ref[parent, 0, group]
+            keys = caches[slot][0, 0, group]
             scores.append(
                 lax.dot_general(
                     query, keys, (((1,), (1,)), ((), ())), preferred_element_type=jnp.float32
@@ -60,11 +59,10 @@
     weight = (cached_exp / denominator).astype(jnp.bfloat16)
     newest_weight = (newest_exp / denominator).astype(jnp.bfloat16).astype(jnp.float32)
     for slot in range(capacity):
-        parent = parent_ref[first + slot]
         parts = []
         for group in range(groups):
             low = (slot * groups + group) * per_group
-            values = cache_ref[parent, 1, group]
+            values = caches[slot][0, 1, group]
             value_row = new_ref[
                 0, slot, head_count + groups + group : head_count + groups + group + 1, :
             ]
@@ -83,7 +81,13 @@
         grid=(device_count,),
         in_specs=[
             pl.BlockSpec((1, capacity, rows, HEAD_DIM), lambda i, *_: (i, 0, 0, 0)),
-            pl.BlockSpec(memory_space=pltpu.VMEM),
+        ]
+        + [
+            pl.BlockSpec(
+                (1,) + cache.shape[1:],
+                lambda i, parents, _, slot=slot: (parents[i * capacity + slot], 0, 0, 0, 0),
+            )
+            for slot in range(capacity)
         ],
         out_specs=pl.BlockSpec((1, capacity, head_count, HEAD_DIM), lambda i, *_: (i, 0, 0, 0)),
     )
@@ -93,9 +97,9 @@
         out_shape=jax.ShapeDtypeStruct(
             (device_count, capacity, head_count, HEAD_DIM), jnp.bfloat16
         ),
-        compiler_params=pltpu.CompilerParams(vmem_limit_bytes=40 * 1024 * 1024),
+        compiler_params=pltpu.CompilerParams(vmem_limit_bytes=56 * 1024 * 1024),
         name="attend",
-    )(parents, lengths, arrived, cache)
+    )(parents, lengths, arrived, *[cache] * capacity)
 
 
 MESH = pl.DeviceIdType.MESH
@@ -178,7 +182,9 @@
     raw,
     packed,
     arrive,
+    ordered,
     load_sems,
+    store_sems,
     slot_send,
     slot_recv,
     blocks,
@@ -260,7 +266,7 @@
                 preferred_element_type=jnp.float32,
             ).astype(jnp.bfloat16)
             for kind in range(kinds):
-                sorted_ref[
+                ordered[
                     beam,
                     kind // sorted_ref.shape[2],
                     kind % sorted_ref.shape[2],
@@ -269,7 +275,22 @@
                 ] = moved[kind * each : (kind + 1) * each]
         return carry
 
-    lax.fori_loop(0, raw.shape[0], sort_beam, 0)
+    beams, chunks = raw.shape[0], product.shape[0]
+    cuts = [0, beams * 5 // 16]
+    cuts += [cuts[1] + (step + 1) * (beams // 2) // chunks for step in range(chunks)]
+    cuts += [beams]
+    stores = []
+
+    def sort_part(part):
+        first, last = cuts[part], cuts[part + 1]
+        lax.fori_loop(first, last, sort_beam, 0)
+        store = pltpu.make_async_copy(
+            ordered.at[first:last], sorted_ref.at[first:last], store_sems.at[part]
+        )
+        store.start()
+        stores.append(store)
+
+    sort_part(0)
     passes = []
     for d in range(1, n):
         moves[d - 1].wait_recv()
@@ -289,7 +310,6 @@
         [(blocks[d].astype(jnp.float32) * gain).astype(jnp.bfloat16) for d in range(n)], axis=0
     )
     width = product.shape[-1]
-    chunks = product.shape[0]
     bufs = (product, half, got, block, landed, (half_send, half_recv, block_send, block_recv))
     seconds = []
     for load in loads[2:]:
@@ -304,7 +324,10 @@
             owner = lax.rem(me - d + n, n)
             product[chunk, owner // 2, lax.rem(owner, 2)] = result[d * rows : (d + 1) * rows]
         seconds.append(scatter_sum(chunk, high, low, partner, peers, bufs))
-    finishes = [second() for second in seconds]
+    finishes = []
+    for chunk in range(chunks):
+        sort_part(chunk + 1)
+        finishes.append(seconds[chunk]())
     cosine, sine = cosine_ref[...], sine_ref[...]
     for chunk in range(chunks):
         total = finishes[chunk]() * inverse
@@ -329,6 +352,7 @@
         copy.start()
         copies.append(copy)
     arrive[me] = packed[me]
+    sort_part(chunks + 1)
     for copy in copies:
         copy.wait_send()
     for d in range(1, n):
@@ -337,6 +361,8 @@
             packed.at[source], arrive.at[source], slot_send.at[d], slot_recv.at[d], (source, rank)
         ).wait_recv()
     out_ref[...] = arrive[...]
+    for store in stores:
+        store.wait()
 
 
 def sum_scratch(chunks, nh, rows, width):
@@ -377,7 +403,7 @@
             jax.ShapeDtypeStruct((beams, 2, groups, length, HEAD_DIM), jnp.bfloat16),
         ],
         in_specs=[hbm, vmem, hbm, hbm, hbm, vmem, vmem, vmem, hbm],
-        out_specs=[vmem, vmem],
+        out_specs=[vmem, hbm],
         scratch_shapes=[
             pltpu.VMEM(hidden.shape, jnp.bfloat16),
             pltpu.VMEM(query_weight.shape, jnp.bfloat16),
@@ -385,7 +411,9 @@
             pltpu.VMEM(flat.shape, jnp.bfloat16),
             pltpu.VMEM((n, capacity, chunks * width), jnp.bfloat16),
             pltpu.VMEM((n, capacity, chunks * width), jnp.bfloat16),
+            pltpu.VMEM((beams, 2, groups, length, HEAD_DIM), jnp.bfloat16),
             pltpu.SemaphoreType.DMA((5,)),
+            pltpu.SemaphoreType.DMA((chunks + 2,)),
             pltpu.SemaphoreType.DMA((n,)),
             pltpu.SemaphoreType.DMA((n,)),
             pltpu.VMEM((n, rows, depth), jnp.bfloat16),

time: 114 us -> 113 us (level); the launches traced: 112 us -> 113 us
  Pallas kernels: 98.5 us -> 100 us
    pallas_call x1, Pallas kernels: 7.32 us -> 14.5 us  [attend(): pl.pallas_call(functools.partial(attend_kernel, capacity, head_count), gr...]
    pallas_call x1, Pallas kernels: 50.1 us -> 45.1 us  [project(): pl.pallas_call(functools.partial(project_kernel, n), out_shape=[jax.Shape...]
    unnamed x5 -> x3, local copies, waits for them, and re-layouts: 5.25 us -> 1.87 us
where the time goes in v4:
time: 113 us
  Pallas kernels  100 us (88%)
  local copies, waits for them, and re-layouts  8.76 us (8%)
  other arithmetic  3.83 us (3%)
    pallas_call x1, Pallas kernels, project(): pl.pallas_call(functools.partial(project_kernel, n), out_shape=[jax.Shape...  45.1 us
    pallas_call x1, Pallas kernels, output(): pl.pallas_call(functools.partial(output_kernel, n, ranks), out_shape=jax....  40.6 us
    pallas_call x1, Pallas kernels, attend(): pl.pallas_call(functools.partial(attend_kernel, capacity, head_count), gr...  14.5 us

profile of v4, /device:TPU:0, one launch (start us, length us, event | category | flops | bytes accessed | tf_op | source)
XLA Modules:
  0.0 112.9 jit_solution(10134853094511907018)
XLA Ops:
  0.0 0.9 select_reduce_fusion
  0.9 0.1 broadcast_in_dim.58
  1.0 0.8 reshape.144
  1.7 0.3 convert_reduce_fusion
  2.1 0.3 select_reduce_fusion.1
  2.4 0.6 reshape.145.parent_ref
  3.0 0.6 reshape.146.length_ref
  3.6 1.3 %broadcast_in_dim.60.gain_ref = bf16[1,1024]{1,0:T(2,128)(2,1)} reshape(bf16[1024]{0:T(1024)(128)(2,1)} %param.11) | data formatting | bytes 4096 | tf_op jit(solution)/shard_map/broadcast_in_dim | solution.py:672
  4.9 0.1 dynamic-slice_convert_fusion
  5.0 0.1 fusion.4
  5.1 0.7 pad_maximum_fusion
  5.8 0.6 fusion.1.placing_ref
  6.4 45.1 %project.1 = (bf16[8,8,2560]{2,1,0:T(8,128)(2,1)}, bf16[32,2,2,256,128]{4,3,2,1,0:T(8,128)(2,1)}) custom-call(bf16[32,8192]{1,0:T(8,128)(2,1)} %hidden_ref.1, bf16[1,1024]{1,0:T(2,128)(2,1)} %broadcast_in_dim.60.gain_ref, bf16[1024,2048]{1,0:T(8,128)(2,1)} %query_ref.1, bf16[1024,256]{1,0:T(8,128)(2,1)} %key_ref.1, bf16[1024,256]{1,0:T(8,128)(2,1)} %value_ref.1, ...), custom_call_target="tpu_custom_call" | custom-call | flops 1342177280 | bytes 8000000 | tf_op jit(solution)/shard_map/project/pallas_call | solution.py:399
  51.5 1.8 %copy.12.new_ref = bf16[8,8,20,128]{3,2,1,0:T(8,128)(2,1)} copy(bf16[8,8,20,128]{3,1,2,0:T(8,128)(2,1)} %bitcast.7) | data formatting | bytes 655360 | tf_op jit(solution)/shard_map/reshape | solution.py:681
  53.3 0.0 copy-start
  53.3 14.5 %attend.1 = bf16[8,8,16,128]{3,2,1,0:T(8,128)(2,1)} custom-call(s32[64]{0:T(128)} %reshape.145.parent_ref, s32[64]{0:T(128)} %reshape.146.length_ref, bf16[8,8,20,128]{3,2,1,0:T(8,128)(2,1)} %copy.12.new_ref, bf16[32,2,2,256,128]{4,3,2,1,0:T(8,128)(2,1)} %get-tuple-element.8.refs_0_.refs_1_.refs_2_.refs_3_.refs_4_.refs_5_.refs_6_.refs_7_, ...), custom_call_target="tpu_custom_call" | custom-call | tf_op jit(solution)/shard_map/attend/pallas_call | solution.py:94
  67.8 1.8 %reshape.149.slots_ref = bf16[8,8,2048]{2,1,0:T(8,128)(2,1)} reshape(bf16[8,8,16,128]{3,2,1,0:T(8,128)(2,1)} %attend.1) | data formatting | bytes 524288 | tf_op jit(solution)/shard_map/reshape | solution.py:685
  69.6 0.0 copy-done
  69.6 0.1 dynamic-slice_compare_fusion
  69.7 0.7 fusion.3.picking_ref
  70.4 40.6 %output.1 = bf16[256,1024]{1,0:T(8,128)(2,1)} custom-call(bf16[8,8,2048]{2,1,0:T(8,128)(2,1)} %reshape.149.slots_ref, bf16[32,64]{1,0:T(8,128)(2,1)} %fusion.3.picking_ref, bf16[2048,1024]{1,0:T(8,128)(2,1)} %weight_ref.1), custom_call_target="tpu_custom_call" | custom-call | flops 1073741824 | bytes 8000000 | tf_op jit(solution)/shard_map/output/pallas_call | solution.py:579
  111.0 1.9 %copy.14 = bf16[256,1024]{1,0:T(8,128)(2,1)} copy(bf16[256,1024]{1,0:T(8,128)(2,1)} %output.1) | data formatting | bytes 1048576
  (5 shorter events, 0.0 us)
Async XLA Ops:
  53.3 16.3 %copy-start = (s32[256]{0:T(256)S(1)}, s32[256]{0:T(256)}, u32[]{:S(2)}) copy-start(s32[256]{0:T(256)} %param.19) | copy-start | bytes 3076

commit v5 on v4

--- a/solution.py
+++ b/solution.py
@@ -23,20 +23,21 @@
     )
 
 
-def attend_kernel(capacity, head_count, parent_ref, length_ref, new_ref, *refs):
-    caches, out_ref = refs[:capacity], refs[capacity]
-    groups = caches[0].shape[2]
+def attend_kernel(capacity, head_count, parent_ref, length_ref, new_ref, cache_ref, out_ref):
+    groups = cache_ref.shape[2]
+    length = cache_ref.shape[3]
     per_group = head_count // groups
     first = pl.program_id(0) * capacity
     score_scale = 1.0 / math.sqrt(HEAD_DIM)
     rows = groups * per_group
     scores, latest, limits = [], [], []
     for slot in range(capacity):
+        parent = parent_ref[first + slot]
         limits.append(jnp.full((rows, 1), length_ref[first + slot], jnp.int32))
         for group in range(groups):
             query = new_ref[0, slot, group * per_group : (group + 1) * per_group, :]
             key_row = new_ref[0, slot, head_count + group : head_count + group + 1, :]
-            keys = caches[slot][0, 0, group]
+            keys = cache_ref[parent, 0, group]
             scores.append(
                 lax.dot_general(
                     query, keys, (((1,), (1,)), ((), ())), preferred_element_type=jnp.float32
@@ -59,10 +60,11 @@
     weight = (cached_exp / denominator).astype(jnp.bfloat16)
     newest_weight = (newest_exp / denominator).astype(jnp.bfloat16).astype(jnp.float32)
     for slot in range(capacity):
+        parent = parent_ref[first + slot]
         parts = []
         for group in range(groups):
             low = (slot * groups + group) * per_group
-            values = caches[slot][0, 1, group]
+            values = cache_ref[parent, 1, group]
             value_row = new_ref[
                 0, slot, head_count + groups + group : head_count + groups + group + 1, :
             ]
@@ -81,13 +83,7 @@
         grid=(device_count,),
         in_specs=[
             pl.BlockSpec((1, capacity, rows, HEAD_DIM), lambda i, *_: (i, 0, 0, 0)),
-        ]
-        + [
-            pl.BlockSpec(
-                (1,) + cache.shape[1:],
-                lambda i, parents, _, slot=slot: (parents[i * capacity + slot], 0, 0, 0, 0),
-            )
-            for slot in range(capacity)
+            pl.BlockSpec(memory_space=pltpu.VMEM),
         ],
         out_specs=pl.BlockSpec((1, capacity, head_count, HEAD_DIM), lambda i, *_: (i, 0, 0, 0)),
     )
@@ -97,9 +93,9 @@
         out_shape=jax.ShapeDtypeStruct(
             (device_count, capacity, head_count, HEAD_DIM), jnp.bfloat16
         ),
-        compiler_params=pltpu.CompilerParams(vmem_limit_bytes=56 * 1024 * 1024),
+        compiler_params=pltpu.CompilerParams(vmem_limit_bytes=40 * 1024 * 1024),
         name="attend",
-    )(parents, lengths, arrived, *[cache] * capacity)
+    )(parents, lengths, arrived, cache)
 
 
 MESH = pl.DeviceIdType.MESH

time: 113 us -> 106 us (0.938); the launches traced: 113 us -> 105 us
  Pallas kernels: 100 us -> 91.2 us
    pallas_call x1, Pallas kernels: 14.5 us -> 7.32 us  [attend(): pl.pallas_call(functools.partial(attend_kernel, capacity, head_count), gr...]
    unnamed x3 -> x5, local copies, waits for them, and re-layouts: 1.87 us -> 5.25 us
    pallas_call x1, Pallas kernels: 40.6 us -> 38.8 us  [output(): pl.pallas_call(functools.partial(output_kernel, n, ranks), out_shape=jax....]
where the time goes in v5:
time: 106 us; the launch traced here: 105 us
  Pallas kernels  91.2 us (86%)
  local copies, waits for them, and re-layouts  9.41 us (9%)
  other arithmetic  3.83 us (4%)
    pallas_call x1, Pallas kernels, project(): pl.pallas_call(functools.partial(project_kernel, n), out_shape=[jax.Shape...  45.1 us
    pallas_call x1, Pallas kernels, output(): pl.pallas_call(functools.partial(output_kernel, n, ranks), out_shape=jax....  38.8 us
    pallas_call x1, Pallas kernels, attend(): pl.pallas_call(functools.partial(attend_kernel, capacity, head_count), gr...  7.32 us
    unnamed x5, local copies, waits for them, and re-layouts  5.25 us

profile of v5, /device:TPU:0, one launch (start us, length us, event | category | flops | bytes accessed | tf_op | source)
XLA Modules:
  0.0 104.6 jit_solution(15366126593377957577)
XLA Ops:
  0.0 0.9 select_reduce_fusion
  0.9 0.1 broadcast_in_dim.58
  1.0 0.8 reshape.144
  1.7 0.3 convert_reduce_fusion
  2.1 0.3 select_reduce_fusion.1
  2.4 0.1 reshape.145.parent_ref
  2.5 0.1 reshape.146.length_ref
  2.6 1.3 %broadcast_in_dim.60.gain_ref = bf16[1,1024]{1,0:T(2,128)(2,1)} reshape(bf16[1024]{0:T(1024)(128)(2,1)} %param.11) | data formatting | bytes 4096 | tf_op jit(solution)/shard_map/broadcast_in_dim | solution.py:668
  3.9 0.1 dynamic-slice_convert_fusion
  3.9 0.1 fusion.4
  4.1 0.7 pad_maximum_fusion
  4.8 0.6 fusion.1.placing_ref
  5.4 45.1 %project.1 = (bf16[8,8,2560]{2,1,0:T(8,128)(2,1)}, bf16[32,2,2,256,128]{4,3,2,1,0:T(8,128)(2,1)}) custom-call(bf16[32,8192]{1,0:T(8,128)(2,1)} %hidden_ref.1, bf16[1,1024]{1,0:T(2,128)(2,1)} %broadcast_in_dim.60.gain_ref, bf16[1024,2048]{1,0:T(8,128)(2,1)} %query_ref.1, bf16[1024,256]{1,0:T(8,128)(2,1)} %key_ref.1, bf16[1024,256]{1,0:T(8,128)(2,1)} %value_ref.1, ...), custom_call_target="tpu_custom_call" | custom-call | flops 1342177280 | bytes 8000000 | tf_op jit(solution)/shard_map/project/pallas_call | solution.py:395
  50.5 0.0 copy-start.1
  50.5 1.0 copy.12.new_ref
  51.6 0.0 copy-start
  51.6 3.4 %copy-done = bf16[32,2,2,256,128]{4,3,2,1,0:T(8,128)(2,1)S(1)} copy-done((bf16[32,2,2,256,128]{4,3,2,1,0:T(8,128)(2,1)S(1)}, bf16[32,2,2,256,128]{4,3,2,1,0:T(8,128)(2,1)}, u32[]{:S(2)}) %copy-start) | copy-done | bytes 8388632
  55.0 7.3 %attend.1 = bf16[8,8,16,128]{3,2,1,0:T(8,128)(2,1)S(1)} custom-call(s32[64]{0:T(128)S(1)} %reshape.145.parent_ref, s32[64]{0:T(128)S(1)} %reshape.146.length_ref, bf16[8,8,20,128]{3,2,1,0:T(8,128)(2,1)S(1)} %copy.12.new_ref, bf16[32,2,2,256,128]{4,3,2,1,0:T(8,128)(2,1)S(1)} %copy-done), custom_call_target="tpu_custom_call" | custom-call | tf_op jit(solution)/shard_map/attend/pallas_call | solution.py:90
  62.3 0.8 reshape.149.slots_ref
  63.1 0.0 copy-done.1
  63.1 0.1 dynamic-slice_compare_fusion
  63.2 0.7 fusion.3.picking_ref
  63.9 38.8 %output.1 = bf16[256,1024]{1,0:T(8,128)(2,1)} custom-call(bf16[8,8,2048]{2,1,0:T(8,128)(2,1)} %reshape.149.slots_ref, bf16[32,64]{1,0:T(8,128)(2,1)} %fusion.3.picking_ref, bf16[2048,1024]{1,0:T(8,128)(2,1)} %weight_ref.1), custom_call_target="tpu_custom_call" | custom-call | flops 1073741824 | bytes 8000000 | tf_op jit(solution)/shard_map/output/pallas_call | solution.py:575
  102.7 1.9 %copy.14 = bf16[256,1024]{1,0:T(8,128)(2,1)} copy(bf16[256,1024]{1,0:T(8,128)(2,1)} %output.1) | data formatting | bytes 1048576
  (5 shorter events, 0.0 us)
Async XLA Ops:
  50.5 12.6 %copy-start.1 = (s32[256]{0:T(256)S(1)}, s32[256]{0:T(256)}, u32[]{:S(2)}) copy-start(s32[256]{0:T(256)} %param.19) | copy-start | bytes 3076
  51.6 3.4 %copy-start = (bf16[32,2,2,256,128]{4,3,2,1,0:T(8,128)(2,1)S(1)}, bf16[32,2,2,256,128]{4,3,2,1,0:T(8,128)(2,1)}, u32[]{:S(2)}) copy-start(bf16[32,2,2,256,128]{4,3,2,1,0:T(8,128)(2,1)} %get-tuple-element.8.cache_ref) | copy-start | bytes 25165828
